TPU v7x, 32 devices: a whole 2x2x4 slice. The times are simulated.
32 devices in a mesh: section: 2 (over core), ctx: 16 (over z, y, x).
Axes of the slice: x: 2, y: 2, z: 4, core: 2. Of those that a mesh axis runs over, the one named last changes fastest.
Arguments:
- tokens: bfloat16 [2, 2048, 1024], P(None, 'ctx'), may hold values from -6 to 6
- cotangent: bfloat16 [2, 2048, 1024], P(None, 'ctx'), may hold values from -6 to 6
- bounds: int32 [2, 8], replicated, may hold values from 0 to 2048, as said below
- norm_gain: bfloat16 [2, 1024], P('section'), may hold values from 0.5 to 1.5
- in_proj: bfloat16 [2, 1024, 4096], P('section'), may hold values from -0.1875 to 0.1875
- conv_kernel: bfloat16 [2, 4, 2048], P('section'), may hold values from -3 to 3
- conv_bias: bfloat16 [2, 2048], P('section'), may hold values from -3 to 3
- x_proj: bfloat16 [2, 2048, 96], P('section'), may hold values from -0.125 to 0.125
- dt_proj: bfloat16 [2, 64, 2048], P('section'), may hold values from -0.75 to 0.75
- dt_bias: bfloat16 [2, 2048], P('section'), may hold values from -9 to 1
- skip_gain: bfloat16 [2, 2048], P('section'), may hold values from 0.5 to 1.5
- out_proj: bfloat16 [2, 2048, 1024], P('section'), may hold values from -0.25 to 0.25
Outputs:
- block_out: bfloat16 [2, 2048, 1024], P('section', 'ctx')
- grad_tokens: bfloat16 [2, 2048, 1024], P('section', 'ctx')
- grad_norm_gain: float32 [2, 1024], P('section', 'ctx')
- grad_in_proj: float32 [2, 1024, 4096], P('section', 'ctx')
- grad_conv_kernel: float32 [2, 4, 2048], P('section', None, 'ctx')
- grad_conv_bias: float32 [2, 2048], P('section', 'ctx')
- grad_x_proj: float32 [2, 2048, 96], P('section', 'ctx')
- grad_dt_proj: float32 [2, 64, 2048], P('section', 'ctx')
- grad_dt_bias: float32 [2, 2048], P('section', 'ctx')
- grad_skip_gain: float32 [2, 2048], P('section', 'ctx')
- grad_out_proj: float32 [2, 2048, 1024], P('section', 'ctx')
Inputs may be any that keep to these rules, and one draw needn't show every extreme that they name: Each row bounds[m] rises strictly from 0 to 2048: seven sequences. In one micro-batch, chosen by the draw, the first three sequences end within the first 128 tokens and the last three start within the last 128 tokens. In every other micro-batch the cuts lie anywhere, and the sequences are four of 128 tokens and three of 512 tokens in some order, with the first one longer and the last one shorter by the same amount, less than 64.
All inputs are finite; a program needn't handle non-finite values.
Results may differ from a plain program's by a relative error of at most 0.023.
Values may be sent and summed in bfloat16 or wider, within the bound.
A program may use at most 256 MiB of HBM per device.

v0:
```python
import math

import jax
import jax.numpy as jnp
from jax import lax
from jax.sharding import PartitionSpec as P

HIGHEST = lax.Precision.HIGHEST
NORM_EPS = 1e-05


def from_behind(value, axis, by):
    size = lax.axis_size(axis)
    pairs = [(i, i + by) for i in range(size) if 0 <= i + by < size]
    return lax.ppermute(value, axis, pairs)


def carried_in(value, axis, combine, identity, reverse):
    size, mine = (lax.axis_size(axis), lax.axis_index(axis))
    everything = jax.tree.map(
        lambda part, kind: lax.all_gather(part.astype(kind), axis),
        value,
        (jnp.bfloat16, jnp.bfloat16),
    )
    start = jax.tree.map(
        lambda part, zero: jnp.broadcast_to(jnp.asarray(zero, part.dtype), part.shape),
        value,
        identity,
    )

    def turn(k, before):
        at = size - 1 - k if reverse else k
        reached = at > mine if reverse else at < mine
        new = combine(
            before, jax.tree.map(lambda part, own: part[at].astype(own.dtype), everything, value)
        )
        return jax.tree.map(lambda a, b: jnp.where(reached, a, b), new, before)

    return lax.fori_loop(0, size, turn, start)


def from_partner(value, axis, bit):
    mask = 2**bit
    pairs = [(source, source ^ mask) for source in range(lax.axis_size(axis))]
    return lax.ppermute(value, axis, pairs)


def silu_grad(values):
    sigmoid_v = jax.nn.sigmoid(values)
    return sigmoid_v * (1.0 + values * (1.0 - sigmoid_v))


def segment_of(position, bounds_row):
    segment = jnp.zeros(position.shape, jnp.int32)
    for cut_index in range(1, 7):
        segment = segment + (position >= bounds_row[cut_index]).astype(jnp.int32)
    return segment


def starts_of(position, bounds_row):
    seq_start = jnp.zeros(position.shape, jnp.int32)
    for cut_index in range(1, 7):
        seq_start = jnp.where(position >= bounds_row[cut_index], bounds_row[cut_index], seq_start)
    return seq_start


def layout_info(bounds_row, row_count, block_len):
    first_row = lax.axis_index("ctx") * row_count
    position = first_row + jnp.arange(row_count, dtype=jnp.int32)
    segment = segment_of(position, bounds_row)
    before = segment_of(first_row - 1, bounds_row)
    previous = jnp.concatenate([before[None], segment[:-1]])
    block_count = row_count // block_len
    seg_blocks = segment.reshape(block_count, block_len)
    carry_mask = (seg_blocks == previous.reshape(block_count, block_len)[:, :1]).astype(jnp.float32)
    lower_tri = jnp.arange(block_len)[:, None] >= jnp.arange(block_len)[None, :]
    same_seq = seg_blocks[:, :, None] == seg_blocks[:, None, :]
    within = (same_seq & lower_tri[None]).astype(jnp.float32)
    device_mask = (segment == before).astype(jnp.float32)
    unbroken = (segment[-1] == before) & (first_row > 0)
    seq_start = starts_of(position, bounds_row)
    return (position, seq_start, carry_mask, within, device_mask, unbroken)


def log_decay(step_blk, key_blk):
    return -(key_blk * key_blk)[:, :, None] * step_blk[:, None, :]


def block_states(carried, pieces):
    step_blk, key_blk, act_blk, query_blk, carry_blk, within_blk = pieces
    cumulative = jnp.cumsum(log_decay(step_blk, key_blk), axis=0)
    source = (step_blk * act_blk)[:, None, :] * key_blk[:, :, None]
    length = cumulative.shape[0]
    inner_sum = jnp.dot(
        within_blk,
        (jnp.exp(-cumulative) * source).reshape(length, -1),
        precision=HIGHEST,
        preferred_element_type=jnp.float32,
    ).reshape(cumulative.shape)
    states = jnp.exp(cumulative) * (inner_sum + carry_blk[:, None, None] * carried[None])
    output = jnp.einsum("tn,tne->te", query_blk, states, precision=HIGHEST)
    return (states[-1], output)


def to_blocks(values, block_len):
    return values.reshape((values.shape[0] // block_len, block_len) + values.shape[1:])


def run_states(
    start_state, step_size, key_vecs, conv_act, query_vecs, carry_mask, within, block_len
):
    pieces = (
        to_blocks(step_size, block_len),
        to_blocks(key_vecs, block_len),
        to_blocks(conv_act, block_len),
        to_blocks(query_vecs, block_len),
        carry_mask,
        within,
    )
    end_state, outputs = lax.scan(jax.checkpoint(block_states), start_state, pieces)
    return (outputs.reshape(step_size.shape), end_state)


def end_summary(step_size, key_vecs, conv_act, carry_mask, within, block_len):

    def end_advance(carry, pieces):
        carried, log_sum = carry
        step_blk, key_blk, act_blk, carry_blk, within_blk = pieces
        cumulative = jnp.cumsum(log_decay(step_blk, key_blk), axis=0)
        source = (step_blk * act_blk)[:, None, :] * key_blk[:, :, None]
        weight = within_blk[-1][:, None, None] * jnp.exp(cumulative[-1][None] - cumulative)
        carried = jnp.exp(cumulative[-1]) * carry_blk[-1] * carried + jnp.sum(
            weight * source, axis=0
        )
        return ((carried, log_sum + cumulative[-1]), None)

    zero_state = jnp.zeros((key_vecs.shape[1], step_size.shape[1]), jnp.float32)
    pieces = (
        to_blocks(step_size, block_len),
        to_blocks(key_vecs, block_len),
        to_blocks(conv_act, block_len),
        carry_mask,
        within,
    )
    (local_end, log_sum), unused = lax.scan(end_advance, (zero_state, zero_state), pieces)
    return (local_end, log_sum)


def start_gradient(step_size, key_vecs, query_vecs, grad_output, device_mask, block_len):

    def start_advance(carry, pieces):
        running, log_sum = carry
        step_blk, key_blk, query_blk, grad_blk, mask_blk = pieces
        cumulative = log_sum[None] + jnp.cumsum(log_decay(step_blk, key_blk), axis=0)
        weight = jnp.exp(cumulative) * mask_blk[:, None, None]
        running = running + jnp.einsum(
            "tne,tn,te->ne", weight, query_blk, grad_blk, precision=HIGHEST
        )
        return ((running, cumulative[-1]), None)

    zero_state = jnp.zeros((key_vecs.shape[1], step_size.shape[1]), jnp.float32)
    pieces = (
        to_blocks(step_size, block_len),
        to_blocks(key_vecs, block_len),
        to_blocks(query_vecs, block_len),
        to_blocks(grad_output, block_len),
        to_blocks(device_mask, block_len),
    )
    (running, unused_sum), unused = lax.scan(start_advance, (zero_state, zero_state), pieces)
    return running


def chain_pair(earlier, later):
    return (earlier[0] * later[0], later[0] * earlier[1] + later[1])


def mixer_forward(hidden, params, layout, block_len):
    norm_gain, in_proj, conv_kernel, conv_bias, x_proj, dt_proj, dt_bias, skip_gain, out_proj = (
        params
    )
    position, seq_start, carry_mask, within, device_mask, unbroken = layout
    tap_count = conv_kernel.shape[0]
    inner_width = conv_kernel.shape[1]
    row_count = hidden.shape[0]
    inv_rms = lax.rsqrt(jnp.mean(hidden * hidden, axis=-1, keepdims=True) + NORM_EPS)
    normed = (hidden * inv_rms * norm_gain.astype(jnp.float32)).astype(jnp.bfloat16)
    mixed_in = jnp.dot(normed, in_proj, preferred_element_type=jnp.float32)
    x_in = mixed_in[:, :inner_width]
    gate_in = mixed_in[:, inner_width:]
    rim_rows = from_behind(x_in[row_count - tap_count + 1 :], "ctx", 1)
    padded = jnp.concatenate([rim_rows, x_in], axis=0)
    valid_taps = jnp.stack(
        [
            (position - (tap_count - 1 - tap_index) >= seq_start).astype(jnp.float32)[:, None]
            for tap_index in range(tap_count)
        ]
    )
    kernel = conv_kernel.astype(jnp.float32)
    conv_pre = conv_bias.astype(jnp.float32) + jnp.zeros_like(x_in)
    for tap_index in range(tap_count):
        conv_pre = (
            conv_pre
            + kernel[tap_index] * padded[tap_index : tap_index + row_count] * valid_taps[tap_index]
        )
    conv_act = jax.nn.silu(conv_pre)
    act_low = conv_act.astype(jnp.bfloat16)
    projected = jnp.dot(act_low, x_proj, preferred_element_type=jnp.float32).astype(jnp.bfloat16)
    rank_width = dt_proj.shape[0]
    state_width = (projected.shape[1] - rank_width) // 2
    dt_in = projected[:, :rank_width]
    key_vecs = projected[:, rank_width : rank_width + state_width].astype(jnp.float32)
    query_vecs = projected[:, rank_width + state_width :].astype(jnp.float32)
    beta_gate = jax.nn.sigmoid(
        jnp.dot(dt_in, dt_proj, preferred_element_type=jnp.float32) + dt_bias.astype(jnp.float32)
    )
    denominator = 1.0 + beta_gate * jnp.sum(key_vecs * key_vecs, axis=-1, keepdims=True)
    step_size = beta_gate / denominator
    local_end, log_sum = end_summary(step_size, key_vecs, conv_act, carry_mask, within, block_len)
    decay_all = jnp.where(unbroken, jnp.exp(log_sum), 0.0)
    unused, start_state = carried_in(
        (decay_all, local_end),
        "ctx",
        chain_pair,
        (jnp.ones_like(log_sum), jnp.zeros_like(log_sum)),
        False,
    )
    return (
        inv_rms,
        normed,
        padded,
        valid_taps,
        conv_pre,
        conv_act,
        act_low,
        dt_in,
        key_vecs,
        query_vecs,
        beta_gate,
        denominator,
        step_size,
        gate_in,
        start_state,
        decay_all,
    )


def layer_forward(hidden, params, layout, block_len):
    (
        inv_rms,
        normed,
        padded,
        valid_taps,
        conv_pre,
        conv_act,
        act_low,
        dt_in,
        key_vecs,
        query_vecs,
        beta_gate,
        denominator,
        step_size,
        gate_in,
        start_state,
        decay_all,
    ) = mixer_forward(hidden, params, layout, block_len)
    output_rec, unused = run_states(
        start_state, step_size, key_vecs, conv_act, query_vecs, layout[2], layout[3], block_len
    )
    output = output_rec + params[7].astype(jnp.float32) * conv_act
    gated = (output * jax.nn.silu(gate_in)).astype(jnp.bfloat16)
    return hidden + jnp.dot(gated, params[8], preferred_element_type=jnp.float32)


def layer_backward(hidden, upstream, params, layout, block_len):
    (
        inv_rms,
        normed,
        padded,
        valid_taps,
        conv_pre,
        conv_act,
        act_low,
        dt_in,
        key_vecs,
        query_vecs,
        beta_gate,
        denominator,
        step_size,
        gate_in,
        start_state,
        decay_all,
    ) = mixer_forward(hidden, params, layout, block_len)
    norm_gain, in_proj, conv_kernel, conv_bias, x_proj, dt_proj, dt_bias, skip_gain, out_proj = (
        params
    )
    carry_mask = layout[2]
    within = layout[3]
    device_mask = layout[4]
    tap_count = conv_kernel.shape[0]
    row_count = hidden.shape[0]
    grad_branch = upstream.astype(jnp.bfloat16)
    grad_gated = jnp.einsum("td,ed->te", grad_branch, out_proj, preferred_element_type=jnp.float32)
    gate_act = jax.nn.silu(gate_in)
    grad_output = grad_gated * gate_act
    from_rows = start_gradient(step_size, key_vecs, query_vecs, grad_output, device_mask, block_len)
    unused, grad_end = carried_in(
        (decay_all, from_rows),
        "ctx",
        chain_pair,
        (jnp.ones_like(from_rows), jnp.zeros_like(from_rows)),
        True,
    )

    def local_run(step_arg, key_arg, act_arg, query_arg):
        return run_states(
            start_state, step_arg, key_arg, act_arg, query_arg, carry_mask, within, block_len
        )

    (output_rec, unused_end), pullback = jax.vjp(
        local_run, step_size, key_vecs, conv_act, query_vecs
    )
    grad_step, grad_keys, grad_act, grad_query = pullback((grad_output, grad_end))
    skip_vals = skip_gain.astype(jnp.float32)
    output = output_rec + skip_vals * conv_act
    gated = (output * gate_act).astype(jnp.bfloat16)
    grad_gate = grad_gated * output * silu_grad(gate_in)
    grad_skip = jnp.sum(grad_output * conv_act, axis=0)
    grad_act = grad_act + grad_output * skip_vals
    inv_square = 1.0 / (denominator * denominator)
    grad_beta = grad_step * inv_square
    grad_keys = grad_keys - 2.0 * key_vecs * jnp.sum(
        grad_step * beta_gate * beta_gate * inv_square, axis=-1, keepdims=True
    )
    grad_pre = (grad_beta * beta_gate * (1.0 - beta_gate)).astype(jnp.bfloat16)
    grad_dt_bias = jnp.sum(grad_pre.astype(jnp.float32), axis=0)
    grad_dt_proj = jnp.einsum("tr,te->re", dt_in, grad_pre, preferred_element_type=jnp.float32)
    grad_dt_in = jnp.einsum("te,re->tr", grad_pre, dt_proj, preferred_element_type=jnp.float32)
    grad_proj = jnp.concatenate([grad_dt_in, grad_keys, grad_query], axis=-1).astype(jnp.bfloat16)
    grad_x_proj = jnp.einsum("te,tc->ec", act_low, grad_proj, preferred_element_type=jnp.float32)
    grad_act = grad_act + jnp.einsum(
        "tc,ec->te", grad_proj, x_proj, preferred_element_type=jnp.float32
    )
    grad_conv = grad_act * silu_grad(conv_pre)
    grad_conv_bias = jnp.sum(grad_conv, axis=0)
    kernel = conv_kernel.astype(jnp.float32)
    grad_kernel = jnp.stack(
        [
            jnp.sum(
                grad_conv * padded[tap_index : tap_index + row_count] * valid_taps[tap_index],
                axis=0,
            )
            for tap_index in range(tap_count)
        ]
    )
    grad_padded = jnp.zeros(padded.shape, jnp.float32)
    for tap_index in range(tap_count):
        grad_padded = grad_padded + jnp.pad(
            kernel[tap_index] * grad_conv * valid_taps[tap_index],
            ((tap_index, tap_count - 1 - tap_index), (0, 0)),
        )
    returned_rim = from_behind(grad_padded[: tap_count - 1], "ctx", -1)
    grad_x_in = grad_padded[tap_count - 1 :] + jnp.pad(
        returned_rim, ((row_count - tap_count + 1, 0), (0, 0))
    )
    grad_mixed = jnp.concatenate([grad_x_in, grad_gate], axis=-1).astype(jnp.bfloat16)
    grad_normed = jnp.einsum("tc,dc->td", grad_mixed, in_proj, preferred_element_type=jnp.float32)
    unit_rows = hidden * inv_rms
    grad_gain = jnp.sum(grad_normed * unit_rows, axis=0)
    grad_unit = grad_normed * norm_gain.astype(jnp.float32)
    grad_hidden = upstream + inv_rms * (
        grad_unit - unit_rows * jnp.mean(grad_unit * unit_rows, axis=-1, keepdims=True)
    )
    smalls = (
        grad_gain,
        grad_kernel,
        grad_conv_bias,
        grad_x_proj,
        grad_dt_proj,
        grad_dt_bias,
        grad_skip,
    )
    return (grad_hidden, smalls, (normed, grad_mixed, gated, grad_branch))


def on_device(
    tokens,
    cotangent,
    bounds,
    norm_gain,
    in_proj,
    conv_kernel,
    conv_bias,
    x_proj,
    dt_proj,
    dt_bias,
    skip_gain,
    out_proj,
):
    params = (
        norm_gain[0],
        in_proj[0],
        conv_kernel[0],
        conv_bias[0],
        x_proj[0],
        dt_proj[0],
        dt_bias[0],
        skip_gain[0],
        out_proj[0],
    )
    section = lax.axis_index("section")
    micro_count = tokens.shape[0]
    row_count = tokens.shape[1]
    model_width = tokens.shape[2]
    block_len = math.gcd(row_count, 32)
    steps_total = micro_count + 1
    received = jnp.zeros((row_count, model_width), jnp.bfloat16)
    kept_inputs = []
    layer_outs = []
    for step_no in range(steps_total):
        micro_id = jnp.clip(step_no - section, 0, micro_count - 1)
        layout = layout_info(bounds[micro_id], row_count, block_len)
        own_rows = tokens[min(step_no, micro_count - 1)]
        hidden = jnp.where(section == 0, own_rows, received).astype(jnp.float32)
        kept_inputs.append(hidden)
        result = layer_forward(hidden, params, layout, block_len).astype(jnp.bfloat16)
        layer_outs.append(result)
        if step_no + 1 < steps_total:
            received = from_behind(result, "section", 1)
    empty_rows = jnp.zeros((row_count, model_width), jnp.float32)
    returned = jnp.zeros((row_count, model_width), jnp.bfloat16)
    small_totals = None
    kept_terms = []
    input_grads = []
    for step_no in range(steps_total):
        micro_id = step_no - 1 + section
        live = ((micro_id >= 0) & (micro_id < micro_count)).astype(jnp.float32)
        layout = layout_info(bounds[jnp.clip(micro_id, 0, micro_count - 1)], row_count, block_len)
        later_in = kept_inputs[step_no + 1] if step_no + 1 < steps_total else empty_rows
        earlier_in = kept_inputs[step_no - 1] if step_no >= 1 else empty_rows
        hidden = jnp.where(section == 1, later_in, earlier_in)
        upstream = jnp.where(
            section == 1, cotangent[min(step_no, micro_count - 1)], returned
        ).astype(jnp.float32)
        grad_hidden, smalls, terms = layer_backward(hidden, upstream, params, layout, block_len)
        if small_totals is None:
            small_totals = [live * member for member in smalls]
        else:
            small_totals = [
                acc_sum + live * member for acc_sum, member in zip(small_totals, smalls)
            ]
        kept_terms.append(terms + (live,))
        grad_low = grad_hidden.astype(jnp.bfloat16)
        input_grads.append(grad_low)
        if step_no + 1 < steps_total:
            returned = from_behind(grad_low, "section", -1)
    payload = jnp.where(section == 0, input_grads[micro_count], layer_outs[1])
    swapped = from_partner(payload, "section", 0)
    block_out = jnp.where(section == 1, layer_outs[micro_count], swapped)
    grad_tokens = jnp.where(section == 0, input_grads[1], swapped)
    grad_in = jnp.zeros(params[1].shape, jnp.float32)
    grad_out = jnp.zeros(params[8].shape, jnp.float32)
    for normed, grad_mixed, gated, grad_branch, live in kept_terms:
        grad_in = grad_in + live * jnp.einsum(
            "td,tc->dc", normed, grad_mixed, preferred_element_type=jnp.float32
        )
        grad_out = grad_out + live * jnp.einsum(
            "te,td->ed", gated, grad_branch, preferred_element_type=jnp.float32
        )
    shares = (
        lax.psum_scatter(small_totals[0], "ctx", scatter_dimension=0, tiled=True),
        lax.psum_scatter(small_totals[1], "ctx", scatter_dimension=1, tiled=True),
        lax.psum_scatter(small_totals[2], "ctx", scatter_dimension=0, tiled=True),
        lax.psum_scatter(small_totals[3], "ctx", scatter_dimension=0, tiled=True),
        lax.psum_scatter(small_totals[4], "ctx", scatter_dimension=0, tiled=True),
        lax.psum_scatter(small_totals[5], "ctx", scatter_dimension=0, tiled=True),
        lax.psum_scatter(small_totals[6], "ctx", scatter_dimension=0, tiled=True),
        lax.psum_scatter(grad_in, "ctx", scatter_dimension=0, tiled=True),
        lax.psum_scatter(grad_out, "ctx", scatter_dimension=0, tiled=True),
    )
    (
        share_gain,
        share_kernel,
        share_bias,
        share_x,
        share_dt,
        share_dt_bias,
        share_skip,
        share_in,
        share_out,
    ) = shares
    return (
        block_out[None],
        grad_tokens[None],
        share_gain[None],
        share_in[None],
        share_kernel[None],
        share_bias[None],
        share_x[None],
        share_dt[None],
        share_dt_bias[None],
        share_skip[None],
        share_out[None],
    )


def solution(mesh):
    placed = (
        P(None, "ctx", None),
        P(None, "ctx", None),
        P(),
        P("section", None),
        P("section", None, None),
        P("section", None, None),
        P("section", None),
        P("section", None, None),
        P("section", None, None),
        P("section", None),
        P("section", None),
        P("section", None, None),
    )
    return jax.shard_map(
        on_device,
        mesh=mesh,
        in_specs=placed,
        out_specs=(
            P("section", "ctx", None),
            P("section", "ctx", None),
            P("section", "ctx"),
            P("section", "ctx", None),
            P("section", None, "ctx"),
            P("section", "ctx"),
            P("section", "ctx", None),
            P("section", "ctx", None),
            P("section", "ctx"),
            P("section", "ctx"),
            P("section", "ctx", None),
        ),
        check_vma=False,
    )
```

profile of v0, /device:TPU:0, one launch (start us, length us, event | category | flops | bytes accessed | tf_op | source)
XLA Modules:
  0.0 3140.9 jit_solution(5232113782078617725)
XLA Ops:
  112.6 54.6 %all-gather.31.cloned.1.call-done = bf16[256,2048]{1,0:T(8,128)(2,1)} async-done(((bf16[16,2048]{1,0:T(8,128)(2,1)}), bf16[256,2048]{1,0:T(8,128)(2,1)}) %all-gather.31.cloned.1.call-update) | async-done | bytes 1048592 | tf_op jit(solution)/shard_map/all_gather | solution.py:21
  167.2 57.4 %all-gather.33.cloned.1.call-done = bf16[256,2048]{1,0:T(8,128)(2,1)} async-done(((bf16[16,2048]{1,0:T(8,128)(2,1)}), bf16[256,2048]{1,0:T(8,128)(2,1)}) %all-gather.33.cloned.1.call-update) | async-done | bytes 1048592 | tf_op jit(solution)/shard_map/all_gather | solution.py:21
  241.5 63.2 %while.393 = (s32[]{:T(128)}, f32[16,2048]{1,0:T(8,128)S(1)}, f32[4,32,2048]{2,1,0:T(8,128)}, f32[4,32,16]{2,1,0:T(8,128)S(1)}, f32[4,32,2048]{2,1,0:T(8,128)S(1...) while((s32[]{:T(128)}, f32[16,2048]{1,0:T(8,128)S(1)}, ...), condition=%wide.region_10.11_spmd, body=%wide.region_8.10_spmd.sunk | while | flops 455148544 | bytes 28480392 | solution.py:120
  408.2 57.3 %all-gather.45.cloned.1.call-done = bf16[256,2048]{1,0:T(8,128)(2,1)} async-done(((bf16[16,2048]{1,0:T(8,128)(2,1)}), bf16[256,2048]{1,0:T(8,128)(2,1)}) %all-gather.45.cloned.1.call-update) | async-done | bytes 1048592 | tf_op jit(solution)/shard_map/all_gather | solution.py:21
  481.4 40.8 %all-gather.47.cloned.1.call-done = bf16[256,2048]{1,0:T(8,128)(2,1)} async-done(((bf16[16,2048]{1,0:T(8,128)(2,1)}), bf16[256,2048]{1,0:T(8,128)(2,1)}) %all-gather.47.cloned.1.call-update) | async-done | bytes 1048592 | tf_op jit(solution)/shard_map/all_gather | solution.py:21
  539.9 68.5 %while.396 = (s32[]{:T(128)}, f32[16,2048]{1,0:T(8,128)S(1)}, f32[4,32,2048]{2,1,0:T(8,128)}, f32[4,16,2048]{2,1,0:T(8,128)}, f32[4,32,16]{2,1,0:T(8,128)S(1)}, ...) while((s32[]{:T(128)}, f32[16,2048]{1,0:T(8,128)S(1)}, ...), condition=%wide.region_48.49_spmd, body=%wide.region_46.48_spmd.sunk | while | flops 455148544 | bytes 28742164 | solution.py:120
  611.9 211.9 %while.397 = (s32[]{:T(128)}, f32[16,2048]{1,0:T(8,128)S(1)}, f32[4,32,2048]{2,1,0:T(8,128)}, f32[4,32,16]{1,0,2:T(4,128)}, f32[4,32,2048]{2,1,0:T(8,128)}, /*in...) while((s32[]{:T(128)}, f32[16,2048]{1,0:T(8,128)S(1)}, ...), condition=%wide.region_57.58_spmd, body=%wide.region_49.57_spmd.sunk | while | flops 916555776 | bytes 62464620 | solution.py:120
  894.1 38.1 %all-gather.35.cloned.1.call-done = bf16[256,2048]{1,0:T(8,128)(2,1)} async-done(((bf16[16,2048]{1,0:T(8,128)(2,1)}), bf16[256,2048]{1,0:T(8,128)(2,1)}) %all-gather.35.cloned.1.call-update) | async-done | bytes 1048592 | tf_op jit(solution)/shard_map/all_gather | solution.py:21
  932.2 57.4 %all-gather.37.cloned.1.call-done = bf16[256,2048]{1,0:T(8,128)(2,1)} async-done(((bf16[16,2048]{1,0:T(8,128)(2,1)}), bf16[256,2048]{1,0:T(8,128)(2,1)}) %all-gather.37.cloned.1.call-update) | async-done | bytes 1048592 | tf_op jit(solution)/shard_map/all_gather | solution.py:21
  1006.5 66.3 %while.394 = (s32[]{:T(128)}, f32[16,2048]{1,0:T(8,128)S(1)}, f32[4,32,2048]{2,1,0:T(8,128)}, f32[4,32,16]{2,1,0:T(8,128)S(1)}, f32[4,32,2048]{2,1,0:T(8,128)S(1...) while((s32[]{:T(128)}, f32[16,2048]{1,0:T(8,128)S(1)}, ...), condition=%wide.region_21.22_spmd, body=%wide.region_19.21_spmd.sunk | while | flops 455148544 | bytes 28480008 | solution.py:120
  1173.4 56.9 %all-gather.51.cloned.1.call-done = bf16[256,2048]{1,0:T(8,128)(2,1)} async-done(((bf16[16,2048]{1,0:T(8,128)(2,1)}), bf16[256,2048]{1,0:T(8,128)(2,1)}) %all-gather.51.cloned.1.call-update) | async-done | bytes 1048592 | tf_op jit(solution)/shard_map/all_gather | solution.py:21
  1246.1 40.8 %all-gather.53.cloned.1.call-done = bf16[256,2048]{1,0:T(8,128)(2,1)} async-done(((bf16[16,2048]{1,0:T(8,128)(2,1)}), bf16[256,2048]{1,0:T(8,128)(2,1)}) %all-gather.53.cloned.1.call-update) | async-done | bytes 1048592 | tf_op jit(solution)/shard_map/all_gather | solution.py:21
  1304.7 71.3 %while.398 = (s32[]{:T(128)}, f32[16,2048]{1,0:T(8,128)S(1)}, f32[4,32,2048]{2,1,0:T(8,128)}, f32[4,16,2048]{2,1,0:T(8,128)}, f32[4,32,16]{2,1,0:T(8,128)S(1)}, ...) while((s32[]{:T(128)}, f32[16,2048]{1,0:T(8,128)S(1)}, ...), condition=%wide.region_75.76_spmd, body=%wide.region_73.75_spmd.sunk | while | flops 455148544 | bytes 28742164 | solution.py:120
  1378.9 212.1 %while.399 = (s32[]{:T(128)}, f32[16,2048]{1,0:T(8,128)S(1)}, f32[4,32,2048]{2,1,0:T(8,128)}, f32[4,32,16]{1,0,2:T(4,128)S(1)}, f32[4,32,2048]{2,1,0:T(8,128)}, ...) while((s32[]{:T(128)}, f32[16,2048]{1,0:T(8,128)S(1)}, ...), condition=%wide.region_84.85_spmd, body=%wide.region_76.84_spmd.sunk | while | flops 916555776 | bytes 62465160 | solution.py:120
  1716.7 56.8 %all-gather.57.cloned.1.call-done = bf16[256,2048]{1,0:T(8,128)(2,1)} async-done(((bf16[16,2048]{1,0:T(8,128)(2,1)}), bf16[256,2048]{1,0:T(8,128)(2,1)}) %all-gather.57.cloned.1.call-update) | async-done | bytes 1048592 | tf_op jit(solution)/shard_map/all_gather | solution.py:21
  1789.3 41.6 %all-gather.59.cloned.1.call-done = bf16[256,2048]{1,0:T(8,128)(2,1)} async-done(((bf16[16,2048]{1,0:T(8,128)(2,1)}), bf16[256,2048]{1,0:T(8,128)(2,1)}) %all-gather.59.cloned.1.call-update) | async-done | bytes 1048592 | tf_op jit(solution)/shard_map/all_gather | solution.py:21
  1848.6 76.8 %while.400 = (s32[]{:T(128)}, f32[16,2048]{1,0:T(8,128)S(1)}, f32[4,32,2048]{2,1,0:T(8,128)}, f32[4,16,2048]{2,1,0:T(8,128)}, f32[4,32,16]{2,1,0:T(8,128)}, /*in...) while((s32[]{:T(128)}, f32[16,2048]{1,0:T(8,128)S(1)}, ...), condition=%wide.region_102.103_spmd, body=%wide.region_100.102_spmd.sunk | while | flops 455148544 | bytes 28742164 | solution.py:120
  1928.8 226.1 %while.401 = (s32[]{:T(128)}, f32[16,2048]{1,0:T(8,128)S(1)}, f32[4,32,2048]{2,1,0:T(8,128)}, f32[4,32,16]{1,0,2:T(4,128)}, f32[4,32,2048]{2,1,0:T(8,128)}, /*in...) while((s32[]{:T(128)}, f32[16,2048]{1,0:T(8,128)S(1)}, ...), condition=%wide.region_111.112_spmd, body=%wide.region_103.111_spmd.sunk | while | flops 916555776 | bytes 63046988 | solution.py:120
  2285.1 74.1 %all-reduce.23 = (f32[1024]{0:T(1024)S(1)}, f32[2048]{0:T(1024)S(1)}, f32[2048]{0:T(1024)S(1)}, f32[2048]{0:T(1024)S(1)}) all-reduce(f32[1024]{0:T(1024)S(1)} %multiply_add_fusion.17, f32[2048]{0:T(1024)S(1)} %multiply_add_fusion.16, f32[2048]{0:T(1024)S(1)} %multiply_add_fusion.15, ...), channel_id=17, replica_groups=mesh['section'=2,'ctx'=16] {'ctx'}, use_global_device_ids=true, to_apply=%region_117.118.clone | all-reduce | flops 7168 | bytes 57344
  2366.2 53.3 %all-gather.39.cloned.1.call-done = bf16[256,2048]{1,0:T(8,128)(2,1)} async-done(((bf16[16,2048]{1,0:T(8,128)(2,1)}), bf16[256,2048]{1,0:T(8,128)(2,1)}) %all-gather.39.cloned.1.call-update) | async-done | bytes 1048592 | tf_op jit(solution)/shard_map/all_gather | solution.py:21
  2419.5 56.7 %all-gather.41.cloned.1.call-done = bf16[256,2048]{1,0:T(8,128)(2,1)} async-done(((bf16[16,2048]{1,0:T(8,128)(2,1)}), bf16[256,2048]{1,0:T(8,128)(2,1)}) %all-gather.41.cloned.1.call-update) | async-done | bytes 1048592 | tf_op jit(solution)/shard_map/all_gather | solution.py:21
  2493.2 71.5 %while.395 = (s32[]{:T(128)}, f32[16,2048]{1,0:T(8,128)S(1)}, f32[4,32,2048]{2,1,0:T(8,128)}, f32[4,32,16]{2,1,0:T(8,128)}, f32[4,32,2048]{2,1,0:T(8,128)S(1)}, ...) while((s32[]{:T(128)}, f32[16,2048]{1,0:T(8,128)S(1)}, ...), condition=%wide.region_32.33_spmd, body=%wide.region_30.32_spmd.sunk | while | flops 455148544 | bytes 28480008 | solution.py:120
  2602.5 179.8 %reduce-scatter.11.cloned.1.call-done = f32[128,1024]{1,0:T(8,128)} async-done(((f32[2048,1024]{1,0:T(8,128)}), f32[128,1024]{1,0:T(8,128)}) %reduce-scatter.11.cloned.1.call-update) | async-done | bytes 524304 | tf_op jit(solution)/shard_map/reduce_scatter | solution.py:478
  2782.3 351.5 %reduce-scatter.7.cloned.1.call-done = f32[64,4096]{1,0:T(8,128)} async-done(((f32[1024,4096]{1,0:T(8,128)}), f32[64,4096]{1,0:T(8,128)}) %reduce-scatter.7.cloned.1.call-update) | async-done | bytes 1048592 | tf_op jit(solution)/shard_map/reduce_scatter | solution.py:477
  (1996 shorter events, 2095.5 us)
Async XLA Ops:
  7.2 160.0 %all-gather.31.cloned.1.call-start = ((), (), s32[]{:S(2)}) async-start(), calls=%async_computation.7 | async-start | bytes 1114112 | tf_op jit(solution)/shard_map/all_gather | solution.py:21
  14.0 80.5 %collective-permute-start = (f32[3,2048]{1,0:T(4,128)S(1)}, f32[3,2048]{1,0:T(4,128)S(1)}, u32[]{:S(2)}, u32[]{:S(2)}) collective-permute-start(f32[3,2048]{1,0:T(4,128)S(1)} %slice.827), channel_id=1, source_target_pairs={{0,1},{1,2},{2,3},{3,4},{4,5},{5,6},{6,7},{7,8},{8,9},{9,10},{10,1... | collective-permute-start | bytes 73736 | tf_op jit(solution)/shard_map/ppermute | solution.py:15
  111.4 113.2 %all-gather.33.cloned.1.call-start = ((), (), s32[]{:S(2)}) async-start(), calls=%async_computation.8 | async-start | bytes 1114112 | tf_op jit(solution)/shard_map/all_gather | solution.py:21
  112.2 296.0 %all-gather.43.cloned.1.call-start = ((), (), s32[]{:S(2)}) async-start(), calls=%async_computation.13 | async-start | bytes 1114112 | tf_op jit(solution)/shard_map/all_gather | solution.py:21
  352.6 112.9 %all-gather.45.cloned.1.call-start = ((), (), s32[]{:S(2)}) async-start(), calls=%async_computation.14 | async-start | bytes 1114112 | tf_op jit(solution)/shard_map/all_gather | solution.py:21
  367.4 154.8 %all-gather.47.cloned.1.call-start = ((), (), s32[]{:S(2)}) async-start(), calls=%async_computation.15 | async-start | bytes 1114112 | tf_op jit(solution)/shard_map/all_gather | solution.py:21
  372.4 559.8 %all-gather.35.cloned.1.call-start = ((), (), s32[]{:S(2)}) async-start(), calls=%async_computation.9 | async-start | bytes 1114112 | tf_op jit(solution)/shard_map/all_gather | solution.py:21
  878.1 111.5 %all-gather.37.cloned.1.call-start = ((), (), s32[]{:S(2)}) async-start(), calls=%async_computation.10 | async-start | bytes 1114112 | tf_op jit(solution)/shard_map/all_gather | solution.py:21
  878.8 294.5 %all-gather.49.cloned.1.call-start = ((), (), s32[]{:S(2)}) async-start(), calls=%async_computation.16 | async-start | bytes 1114112 | tf_op jit(solution)/shard_map/all_gather | solution.py:21
  1079.4 10.5 collective-permute-start.7
  1117.2 113.1 %all-gather.51.cloned.1.call-start = ((), (), s32[]{:S(2)}) async-start(), calls=%async_computation.17 | async-start | bytes 1114112 | tf_op jit(solution)/shard_map/all_gather | solution.py:21
  1131.9 155.0 %all-gather.53.cloned.1.call-start = ((), (), s32[]{:S(2)}) async-start(), calls=%async_computation.18 | async-start | bytes 1114112 | tf_op jit(solution)/shard_map/all_gather | solution.py:21
  1139.7 577.0 %all-gather.55.cloned.1.call-start = ((), (), s32[]{:S(2)}) async-start(), calls=%async_computation.19 | async-start | bytes 1114112 | tf_op jit(solution)/shard_map/all_gather | solution.py:21
  1661.4 112.0 %all-gather.57.cloned.1.call-start = ((), (), s32[]{:S(2)}) async-start(), calls=%async_computation.20 | async-start | bytes 1114112 | tf_op jit(solution)/shard_map/all_gather | solution.py:21
  1691.0 139.9 %all-gather.59.cloned.1.call-start = ((), (), s32[]{:S(2)}) async-start(), calls=%async_computation.21 | async-start | bytes 1114112 | tf_op jit(solution)/shard_map/all_gather | solution.py:21
  1707.9 467.4 %collective-permute-start.4 = (f32[3,2048]{1,0:T(4,128)}, f32[3,2048]{1,0:T(4,128)}, u32[]{:S(2)}, u32[]{:S(2)}) collective-permute-start(f32[3,2048]{1,0:T(4,128)} %slice.850), channel_id=1, source_target_pairs={{0,1},{1,2},{2,3},{3,4},{4,5},{5,6},{6,7},{7,8},{8,9},{9,10},{10,1... | collective-permute-start | bytes 73736 | tf_op jit(solution)/shard_map/ppermute | solution.py:15
  1714.2 647.4 %reduce-scatter.13.cloned.1.call-start = ((), (), s32[]{:S(2)}) async-start(), calls=%async_computation.22 | async-start | bytes 1114112
  2175.3 189.4 %all-reduce.26.cloned.1.call-start = ((), (), s32[]{:S(2)}) async-start(), calls=%async_computation.23 | async-start | bytes 1048576
  2184.4 235.1 %all-gather.39.cloned.1.call-start = ((), (), s32[]{:S(2)}) async-start(), calls=%async_computation.11 | async-start | bytes 1114112 | tf_op jit(solution)/shard_map/all_gather | solution.py:21
  2216.7 259.5 %all-gather.41.cloned.1.call-start = ((), (), s32[]{:S(2)}) async-start(), calls=%async_computation.12 | async-start | bytes 1114112 | tf_op jit(solution)/shard_map/all_gather | solution.py:21
  2218.3 384.2 %reduce-scatter.9.cloned.1.call-start = ((), (), s32[]{:S(2)}) async-start(), calls=%async_computation.5 | async-start | bytes 835584 | tf_op jit(solution)/shard_map/reduce_scatter | solution.py:473
  2221.6 560.7 %reduce-scatter.11.cloned.1.call-start = ((), (), s32[]{:S(2)}) async-start(), calls=%async_computation.6 | async-start | bytes 8912896 | tf_op jit(solution)/shard_map/reduce_scatter | solution.py:478
  2231.5 902.4 %reduce-scatter.7.cloned.1.call-start = ((), (), s32[]{:S(2)}) async-start(), calls=%async_computation.4 | async-start | bytes 17825792 | tf_op jit(solution)/shard_map/reduce_scatter | solution.py:477
  2285.1 78.0 %collective-permute-start.13 = (bf16[128,1024]{1,0:T(8,128)(2,1)}, bf16[128,1024]{1,0:T(8,128)(2,1)S(1)}, u32[]{:S(2)}, u32[]{:S(2)}) collective-permute-start(bf16[128,1024]{1,0:T(8,128)(2,1)} %fusion.458), channel_id=1, source_target_pairs={{0,16},{16,0},{1,17},{17,1},{2,18},{18,2},{3,19},{19,3},{4,20},{20... | collective-permute-start | bytes 786440 | tf_op jit(solution)/shard_map/ppermute | solution.py:45
  (294 other events, 5574.1 us)
Sparse Core Ops, SparseCore 0:
  111.6 55.5 all-gather.30
  170.5 54.0 all-gather.32
  352.7 55.4 all-gather.42
  411.4 54.0 all-gather.44
  468.1 54.0 all-gather.46
  878.2 53.9 all-gather.34
  935.5 54.0 all-gather.36
  1117.3 56.0 all-gather.48
  1176.1 54.0 all-gather.50
  1232.8 54.0 all-gather.52
  1661.5 55.1 all-gather.54
  1719.3 54.0 all-gather.56
  1776.8 54.0 all-gather.58
  2175.4 76.4 reduce-scatter.12
  2257.7 104.8 all-reduce.25
  2365.2 54.2 all-gather.38
  2422.1 54.0 all-gather.40
  2481.4 121.1 reduce-scatter.8
  2605.4 176.8 reduce-scatter.10
  2785.0 348.7 reduce-scatter.6
where the time goes:
time: 3170 us; the launch traced here: 3140 us
  waiting for transfers between devices  1260 us (40%)
  matrix products  744 us (23%)
  other arithmetic  616 us (19%)
  local copies, waits for them, and re-layouts  270 us (9%)
  loops' own time  90.9 us (3%)
  blocking collectives  74.1 us (2%)
  between operations  46.6 us (1%)
  starting transfers between devices  36.1 us (1%)
    all_gather x15, waiting for transfers between devices, carried_in(): lax.all_gather(part.astype(kind), axis)  684 us
    dot_general x48, matrix products, block_states(): jnp.dot(within_blk, (jnp.exp(-cumulative) * source).reshape(length, -1),...  398 us
    reduce_scatter x1, waiting for transfers between devices, on_device(): lax.psum_scatter(grad_in, 'ctx', scatter_dimension=0, tiled=True)  352 us
    dot_general x36, matrix products, block_states(): output = jnp.einsum('tn,tne->te', query_blk, states, precision=HIGHEST)  193 us
    another operation x48, other arithmetic, block_states(): cumulative = jnp.cumsum(log_decay(step_blk, key_blk), axis=0)  188 us
    reduce_scatter x1, waiting for transfers between devices, on_device(): lax.psum_scatter(grad_out, 'ctx', scatter_dimension=0, tiled=True)  180 us
    select_n x144, other arithmetic, turn(): return jax.tree.map(lambda a, b: jnp.where(reached, a, b), new, before)  139 us
    another operation x9, loops' own time, run_states(): lax.scan(jax.checkpoint(block_states), start_state, pieces)  85.5 us
  transfers between devices with their start and end apart: 34, of which 23 were waited for; matrix products, arithmetic and copies ran while one was open for 23% of the time, Pallas kernels for 0%

commit v1 on v0

v1 whole, which is shorter than its diff:
```python
import functools
import math

import jax
import jax.numpy as jnp
from jax import lax
from jax.experimental import pallas as pl
from jax.experimental.pallas import tpu as pltpu
from jax.sharding import PartitionSpec as P

NORM_EPS = 1e-05
LOG2E = math.log2(math.e)
BF = jnp.bfloat16
F32 = jnp.float32
MESH = pl.DeviceIdType.MESH
LANES = 128
BT = 16
N = 16
MIB = 2**20
VSPEC = pl.BlockSpec(memory_space=pltpu.VMEM)
ANYSPEC = pl.BlockSpec(memory_space=pl.ANY)


def params(**kw):
    return pltpu.CompilerParams(vmem_limit_bytes=56 * MIB, **kw)


def dot(a, b):
    return jnp.dot(a, b, preferred_element_type=F32)


def dot_nt(a, b):
    return lax.dot_general(a, b, (((1,), (1,)), ((), ())), preferred_element_type=F32)


def dot_tn(a, b):
    return lax.dot_general(a, b, (((0,), (0,)), ((), ())), preferred_element_type=F32)


def iota(shape, dim):
    return lax.broadcasted_iota(jnp.int32, shape, dim)


def chosen_copy(layer, own, other, dst, sem):
    sec = lax.axis_index("section")

    @pl.when(sec == layer)
    def _():
        pltpu.make_async_copy(own, dst, sem).start()

    @pl.when(sec != layer)
    def _():
        pltpu.make_async_copy(other, dst, sem).start()


def wait_copy(src, dst, sem):
    pltpu.make_async_copy(src, dst, sem).wait()


def silu_parts(v):
    s = jax.nn.sigmoid(v)
    return v * s, s * (1.0 + v * (1.0 - s))


def fwd_a_kernel(
    layer, rank, h_ref, rim_ref, gain_ref, ck_ref, cb_ref, xp_ref, dtp_ref, dtb_ref, mask_ref,
    in_own, in_oth,
    u_ref, xi_ref, z_ref, c_ref, proj_ref, beta_ref, ex_ref, us_ref, k2_ref, kb_ref, qb_ref, summ_ref,
    w_buf, sems,
):
    t_len, width = h_ref.shape
    inner = z_ref.shape[1]
    cb = 512
    n_chunk = 2 * inner // cb
    rim = rim_ref.shape[0]
    for k in range(n_chunk):
        at = pl.ds(k * cb, cb)
        chosen_copy(layer, in_own.at[:, at], in_oth.at[:, at], w_buf.at[:, at], sems.at[k])
    hf = jnp.concatenate([rim_ref[...], h_ref[...]], axis=0).astype(F32)
    inv = lax.rsqrt(jnp.mean(hf * hf, axis=-1, keepdims=True) + NORM_EPS)
    u_all = (hf * inv * gain_ref[...]).astype(BF)
    u_ref[...] = u_all[rim:]
    mask = mask_ref[...]
    proj = jnp.zeros((t_len, LANES), F32)
    for k in range(inner // cb):
        at = pl.ds(k * cb, cb)
        wait_copy(in_own.at[:, at], w_buf.at[:, at], sems.at[k])
        xi = dot(u_all, w_buf[:, at])
        xi_ref[:, at] = xi
        c = cb_ref[:, at] + ck_ref[3:4, at] * xi[rim:]
        for j in range(3):
            c = c + ck_ref[j : j + 1, at] * xi[rim - 3 + j : rim - 3 + j + t_len] * mask[:, j : j + 1]
        c_ref[:, at] = c
        xc = c * jax.nn.sigmoid(c)
        us_ref[:, at] = xc
        proj = proj + dot(xc.astype(BF), xp_ref[at, :])
    cols = iota((t_len, LANES), 1)
    keep = mask[:, 4:5]
    projb = jnp.where(cols == rank + 2 * N, keep, proj).astype(BF)
    proj_ref[...] = projb
    pf = projb.astype(F32)
    ksum = jnp.sum(jnp.where((cols >= rank) & (cols < rank + N), pf * pf, 0.0), axis=-1, keepdims=True)
    for k in range(inner // cb):
        at = pl.ds(k * cb, cb)
        beta = jax.nn.sigmoid(dot(projb, dtp_ref[:, at]) + dtb_ref[:, at])
        eps = beta / (1.0 + beta * ksum)
        beta_ref[:, at] = beta
        us_ref[:, at] = us_ref[:, at] * eps
        ex_ref[:, at] = jnp.where(keep > 0.0, eps, 1.0)
    rows = t_len * N
    sel = (iota((rows, t_len), 0) // N == iota((rows, t_len), 1)).astype(F32).astype(BF)
    spread = dot(sel, projb).astype(BF)
    rn = iota((rows, LANES), 0) % N
    cl = iota((rows, LANES), 1)
    ones = jnp.ones((LANES, LANES), BF)
    zero = jnp.zeros((rows, LANES), BF)
    kb = dot(jnp.where(cl == rank + rn, spread, zero), ones)
    qb = dot(jnp.where(cl == rank + N + rn, spread, zero), ones)
    keepb = dot(jnp.where(cl == rank + 2 * N, spread, zero), ones)
    kb_ref[...] = kb
    qb_ref[...] = qb
    k2_ref[...] = jnp.where(keepb > 0.5, -LOG2E * kb * kb, -1e30)
    ec = 512
    nt = ec // LANES
    un = 8

    def chunk(ci, carry):
        e0 = pl.multiple_of(ci * ec, ec)

        def body(i, sd):
            s, d = [list(v) for v in sd]
            g0 = pl.multiple_of(i * un, un)
            for t in range(un):
                r = pl.multiple_of(g0 * N + t * N, N)
                k2 = k2_ref[pl.ds(r, N), :]
                kv = kb_ref[pl.ds(r, N), :]
                for j in range(nt):
                    lane = pl.ds(e0 + LANES * j, LANES)
                    a = jnp.exp2(k2 * ex_ref.at[pl.ds(g0, un), lane][t : t + 1, :])
                    s[j] = a * s[j] + kv * us_ref.at[pl.ds(g0, un), lane][t : t + 1, :]
                    d[j] = a * d[j]
            return tuple(s), tuple(d)

        zeros = tuple(jnp.zeros((N, LANES), F32) for _ in range(nt))
        one = tuple(jnp.ones((N, LANES), F32) for _ in range(nt))
        s, d = lax.fori_loop(0, t_len // un, body, (zeros, one))
        for j in range(nt):
            lane = pl.ds(e0 + LANES * j, LANES)
            summ_ref[0:N, lane] = d[j].astype(BF)
            summ_ref[N : 2 * N, lane] = s[j].astype(BF)
        return carry

    lax.fori_loop(0, inner // ec, chunk, 0)
    for k in range(inner // cb, n_chunk):
        at = pl.ds(k * cb, cb)
        wait_copy(in_own.at[:, at], w_buf.at[:, at], sems.at[k])
        z_ref[:, pl.ds(k * cb - inner, cb)] = dot(u_all[rim:], w_buf[:, at])


def fwd_a(layer, rank, h, rim, w, mask, in_own, in_oth):
    t_len, width = h.shape
    inner = w["cb"].shape[1]
    rows = t_len * N

    def f32(*s):
        return jax.ShapeDtypeStruct(s, F32)

    def b16(*s):
        return jax.ShapeDtypeStruct(s, BF)

    return pl.pallas_call(
        functools.partial(fwd_a_kernel, layer, rank),
        out_shape=[
            b16(t_len, width), f32(t_len + rim.shape[0], inner), f32(t_len, inner), f32(t_len, inner),
            b16(t_len, LANES), f32(t_len, inner), f32(t_len, inner), f32(t_len, inner),
            f32(rows, LANES), f32(rows, LANES), f32(rows, LANES), b16(2 * N, inner),
        ],
        in_specs=[VSPEC] * 9 + [ANYSPEC] * 2,
        out_specs=[VSPEC] * 12,
        scratch_shapes=[pltpu.VMEM((width, 2 * inner), BF), pltpu.SemaphoreType.DMA((2 * inner // 512,))],
        compiler_params=params(),
        name=f"fwd_in_{layer}",
    )(h, rim, w["gain"], w["ck"], w["cb"], w["xp"], w["dtp"], w["dtb"], mask, in_own, in_oth)


def carry_kernel(n, reverse, *refs):
    if reverse:
        s_ref, d_ref, in_ref, recv, pre, send1, recv1, send2, recv2 = refs
        parts = 1
    else:
        s_ref, in_ref, d_ref, recv, pre, send1, recv1, send2, recv2 = refs
        parts = 2
    inner = s_ref.shape[1]
    blocks = min(n, inner // LANES)
    stride = n // blocks
    sec = lax.axis_index("section")
    me = lax.axis_index("ctx")
    mine = me // stride
    owner = lax.rem(me, stride) == 0

    def when(cond, fn):
        if stride == 1:
            fn()
        else:
            pl.when(cond)(fn)

    def peers(k):
        to = lax.rem(me + k, n)
        frm = lax.rem(me - k + n, n)
        return to, frm

    def first(k):
        to, frm = peers(k)
        lane = pl.ds(pl.multiple_of((to // stride) * LANES, LANES), LANES)
        return pltpu.make_async_remote_copy(
            src_ref=s_ref.at[:, lane], dst_ref=recv.at[me],
            send_sem=send1.at[k], recv_sem=recv1.at[me],
            device_id=(sec, to), device_id_type=MESH)

    def second(k):
        to, frm = peers(k)
        lane = pl.ds(pl.multiple_of(mine * LANES, LANES), LANES)
        return pltpu.make_async_remote_copy(
            src_ref=pre.at[to], dst_ref=in_ref.at[:, lane],
            send_sem=send2.at[k], recv_sem=recv2.at[me],
            device_id=(sec, to), device_id_type=MESH)

    barrier = pltpu.get_barrier_semaphore()
    for k in range(1, n):
        pl.semaphore_signal(barrier, inc=1, device_id=(sec, peers(k)[0]), device_id_type=MESH)
    pl.semaphore_wait(barrier, n - 1)
    for k in range(1, n):
        when(lax.rem(peers(k)[0], stride) == 0, lambda k=k: first(k).start())

    def own_part():
        lane = pl.ds(pl.multiple_of(mine * LANES, LANES), LANES)
        recv[me] = s_ref[:, lane]
        for k in range(1, n):
            frm = peers(k)[1]
            pltpu.make_async_remote_copy(
                src_ref=s_ref.at[:, pl.ds(0, LANES)], dst_ref=recv.at[frm],
                send_sem=send1.at[k], recv_sem=recv1.at[frm],
                device_id=(sec, frm), device_id_type=MESH).wait_recv()
        run = jnp.zeros((N, LANES), F32)
        for i in range(n):
            d = n - 1 - i if reverse else i
            pre[d] = run.astype(BF)
            if reverse:
                dec, st = d_ref[d], recv[d]
            else:
                dec, st = recv[d, 0:N, :], recv[d, N : 2 * N, :]
                d_ref[d] = dec
            run = dec.astype(F32) * run + st.astype(F32)
        for k in range(1, n):
            second(k).start()
        in_ref[:, lane] = pre[me]

    when(owner, own_part)
    for k in range(1, n):
        frm = peers(k)[1]

        def get(frm=frm, k=k):
            lane = pl.ds(pl.multiple_of((frm // stride) * LANES, LANES), LANES)
            pltpu.make_async_remote_copy(
                src_ref=pre.at[0], dst_ref=in_ref.at[:, lane],
                send_sem=send2.at[k], recv_sem=recv2.at[frm],
                device_id=(sec, frm), device_id_type=MESH).wait_recv()

        when(lax.rem(frm, stride) == 0, get)
    for k in range(1, n):
        when(lax.rem(peers(k)[0], stride) == 0, lambda k=k: first(k).wait_send())

    def sent():
        for k in range(1, n):
            second(k).wait_send()

    when(owner, sent)


def carry(n, reverse, cid, summ, decay=None):
    inner = summ.shape[1]
    got = jax.ShapeDtypeStruct((N, inner), BF)
    dec = jax.ShapeDtypeStruct((n, N, LANES), BF)
    rows = N if reverse else 2 * N
    sems = [pltpu.SemaphoreType.DMA((n,))] * 4
    return pl.pallas_call(
        functools.partial(carry_kernel, n, reverse),
        out_shape=[got] if reverse else [got, dec],
        in_specs=[VSPEC] * (2 if reverse else 1),
        out_specs=[VSPEC] * (1 if reverse else 2),
        scratch_shapes=[pltpu.VMEM((n, rows, LANES), BF), pltpu.VMEM((n, N, LANES), BF)] + sems,
        compiler_params=params(collective_id=cid, has_side_effects=True),
        name=f"carry_{cid}",
    )(*((summ, decay) if reverse else (summ,)))


def block_diag(projb, first_col):
    pick = (iota((LANES, BT * N), 0) == first_col + iota((LANES, BT * N), 1) % N).astype(F32).astype(BF)
    vals = dot(projb, pick)
    same = iota((BT, BT * N), 0) == iota((BT, BT * N), 1) // N
    return jnp.where(same, vals, 0.0)


def fwd_b_kernel(
    layer, rank, k2_ref, kb_ref, proj_ref, ex_ref, us_ref, c_ref, z_ref, skip_ref, sin_ref, h_ref, out_own, out_oth,
    s_ref, sb_ref, y_ref, o_ref, hout_ref,
    st, o_all, w_buf, sem,
):
    i = pl.program_id(0)
    inner = z_ref.shape[1]
    ec = 512
    nt = ec // LANES

    @pl.when(i == 0)
    def _():
        chosen_copy(layer, out_own, out_oth, w_buf, sem)
        st[...] = sin_ref[...].astype(F32)

    sb_ref[...] = st[...].astype(BF)
    qbd = block_diag(proj_ref[...], rank + N).astype(BF)
    for ci in range(inner // ec):
        e0 = ci * ec
        s = [st[:, pl.ds(e0 + LANES * j, LANES)] for j in range(nt)]
        for t in range(BT):
            k2 = k2_ref[t * N : (t + 1) * N, :]
            kv = kb_ref[t * N : (t + 1) * N, :]
            for j in range(nt):
                lane = pl.ds(e0 + LANES * j, LANES)
                a = jnp.exp2(k2 * ex_ref[t : t + 1, lane])
                s[j] = a * s[j] + kv * us_ref[t : t + 1, lane]
                s_ref[t * N : (t + 1) * N, lane] = s[j].astype(BF)
        for j in range(nt):
            st[:, pl.ds(e0 + LANES * j, LANES)] = s[j]
        at = pl.ds(e0, ec)
        c = c_ref[:, at]
        y = dot(qbd, s_ref[:, at]) + skip_ref[:, at] * (c * jax.nn.sigmoid(c))
        y_ref[:, at] = y
        z = z_ref[:, at]
        o = (y * (z * jax.nn.sigmoid(z))).astype(BF)
        o_ref[:, at] = o
        o_all[pl.ds(pl.multiple_of(i * BT, BT), BT), at] = o

    @pl.when(i == pl.num_programs(0) - 1)
    def _():
        wait_copy(out_own, w_buf, sem)
        hout_ref[...] = (h_ref[...].astype(F32) + dot(o_all[...], w_buf[...])).astype(BF)


def fwd_b(layer, rank, h, fa, sin, w, out_own, out_oth):
    t_len, width = h.shape
    inner = w["cb"].shape[1]

    def blk(r, c):
        return pl.BlockSpec((r, c), lambda i: (i, 0))

    def whole(r, c):
        return pl.BlockSpec((r, c), lambda i: (0, 0))

    return pl.pallas_call(
        functools.partial(fwd_b_kernel, layer, rank),
        grid=(t_len // BT,),
        in_specs=[
            blk(BT * N, LANES), blk(BT * N, LANES), blk(BT, LANES), blk(BT, inner), blk(BT, inner), blk(BT, inner),
            blk(BT, inner), whole(1, inner), whole(N, inner), whole(t_len, width), ANYSPEC, ANYSPEC,
        ],
        out_specs=[blk(BT * N, inner), blk(BT, inner), blk(BT, inner), blk(BT, inner), whole(t_len, width)],
        out_shape=[
            jax.ShapeDtypeStruct((t_len * N, inner), BF), jax.ShapeDtypeStruct((t_len, inner), BF),
            jax.ShapeDtypeStruct((t_len, inner), F32), jax.ShapeDtypeStruct((t_len, inner), BF),
            jax.ShapeDtypeStruct((t_len, width), BF),
        ],
        scratch_shapes=[
            pltpu.VMEM((N, inner), F32), pltpu.VMEM((t_len, inner), BF), pltpu.VMEM((inner, width), BF),
            pltpu.SemaphoreType.DMA(()),
        ],
        compiler_params=params(),
        name=f"fwd_out_{layer}",
    )(fa["k2"], fa["kb"], fa["proj"], fa["ex"], fa["us"], fa["c"], fa["z"], w["skip"], sin, h, out_own, out_oth)


def bwd_a_kernel(
    layer, gout_ref, z_ref, y_ref, c_ref, o_ref, u_ref, skip_ref, k2_ref, qb_ref, ex_ref, out_own, out_oth,
    dy_ref, dz_ref, go_ref, gz_ref, gskip_ref, from_ref,
    w_buf, sems,
):
    t_len, width = gout_ref.shape
    inner = z_ref.shape[1]
    cb = 512
    for k in range(inner // cb):
        at = pl.ds(k * cb, cb)
        chosen_copy(layer, out_own.at[at, :], out_oth.at[at, :], w_buf.at[at, :], sems.at[k])
    dr = gout_ref[...]
    u = u_ref[...]
    for k in range(inner // cb):
        at = pl.ds(k * cb, cb)
        wait_copy(out_own.at[at, :], w_buf.at[at, :], sems.at[k])
        do = dot_nt(dr, w_buf[at, :])
        act, der = silu_parts(z_ref[:, at])
        dy = do * act
        dy_ref[:, at] = dy
        dz = (do * y_ref[:, at] * der).astype(BF)
        dz_ref[:, at] = dz
        c = c_ref[:, at]
        gskip_ref[:, at] = jnp.sum(dy * (c * jax.nn.sigmoid(c)), axis=0, keepdims=True)
        go_ref[at, :] = dot_tn(o_ref[:, at], dr).astype(BF)
        gz_ref[:, at] = dot_tn(u, dz).astype(BF)
    ec = 512
    nt = ec // LANES
    un = 8

    def chunk(ci, carry):
        e0 = pl.multiple_of(ci * ec, ec)

        def body(i, b):
            b = list(b)
            g0 = pl.multiple_of((t_len // un - 1 - i) * un, un)
            for t in range(un - 1, -1, -1):
                r = pl.multiple_of(g0 * N + t * N, N)
                k2 = k2_ref[pl.ds(r, N), :]
                qv = qb_ref[pl.ds(r, N), :]
                for j in range(nt):
                    lane = pl.ds(e0 + LANES * j, LANES)
                    a = jnp.exp2(k2 * ex_ref.at[pl.ds(g0, un), lane][t : t + 1, :])
                    b[j] = a * (qv * dy_ref.at[pl.ds(g0, un), lane][t : t + 1, :] + b[j])
            return tuple(b)

        b = lax.fori_loop(0, t_len // un, body, tuple(jnp.zeros((N, LANES), F32) for _ in range(nt)))
        for j in range(nt):
            from_ref[:, pl.ds(e0 + LANES * j, LANES)] = b[j].astype(BF)
        return carry

    lax.fori_loop(0, inner // ec, chunk, 0)


def bwd_a(layer, gout, fa, fb, w, out_own, out_oth):
    t_len, width = gout.shape
    inner = w["cb"].shape[1]

    def sd(t, *s):
        return jax.ShapeDtypeStruct(s, t)

    return pl.pallas_call(
        functools.partial(bwd_a_kernel, layer),
        out_shape=[
            sd(F32, t_len, inner), sd(BF, t_len, inner), sd(BF, inner, width), sd(BF, width, inner), sd(F32, 1, inner),
            sd(BF, N, inner),
        ],
        in_specs=[VSPEC] * 10 + [ANYSPEC] * 2,
        out_specs=[VSPEC] * 6,
        scratch_shapes=[pltpu.VMEM((inner, width), BF), pltpu.SemaphoreType.DMA((inner // 512,))],
        compiler_params=params(),
        name=f"back_out_{layer}",
    )(gout, fa["z"], fb["y"], fa["c"], fb["o"], fa["u"], w["skip"], fa["k2"], fa["qb"], fa["ex"], out_own, out_oth)


def bwd_b_kernel(
    rank, k2_ref, qb_ref, proj_blk, ex_ref, us_ref, dy_ref, beta_ref, c_ref, s_ref, sb_ref,
    bin_ref, proj_ref, skip_ref, beta_all, c_all, xi_ref, ck_ref, xp_ref, dtp_ref, mask_ref,
    dxi_ref, rim_ref, gdt_ref, gdtb_ref, gxp_ref, gcb_ref, gck_ref,
    bst, qs, ws, deps_ref, dxc_ref, dkq_ref, dp_ref,
):
    i = pl.program_id(0)
    steps = pl.num_programs(0)
    blk = steps - 1 - i
    t_len = proj_ref.shape[0]
    inner = skip_ref.shape[1]
    ec = 512
    nt = ec // LANES

    @pl.when(i == 0)
    def _():
        bst[...] = bin_ref[...].astype(F32)

    projb = proj_blk[...]
    pf = projb.astype(F32)
    cols = iota((BT, LANES), 1)
    is_k = (cols >= rank) & (cols < rank + N)
    ksum = jnp.sum(jnp.where(is_k, pf * pf, 0.0), axis=-1, keepdims=True)
    kbd = block_diag(projb, rank)
    k2bd = (kbd * kbd).astype(BF)
    kbd = kbd.astype(BF)
    r1 = jnp.zeros((BT, BT * N), F32)
    r2 = jnp.zeros((BT, BT * N), F32)
    r3 = jnp.zeros((BT, BT * N), F32)
    base = pl.multiple_of(blk * BT, BT)
    for ci in range(inner // ec):
        e0 = ci * ec
        b = [bst[:, pl.ds(e0 + LANES * j, LANES)] for j in range(nt)]
        for t in range(BT - 1, -1, -1):
            row = slice(t * N, (t + 1) * N)
            k2 = k2_ref[row, :]
            qv = qb_ref[row, :]
            for j in range(nt):
                lane = pl.ds(e0 + LANES * j, LANES)
                a = jnp.exp2(k2 * ex_ref[t : t + 1, lane])
                q = qv * dy_ref[t : t + 1, lane] + b[j]
                b[j] = a * q
                prev = (s_ref[(t - 1) * N : t * N, lane] if t > 0 else sb_ref[:, lane]).astype(F32)
                qs[row, lane] = q.astype(BF)
                ws[row, lane] = (b[j] * prev).astype(BF)
        for j in range(nt):
            bst[:, pl.ds(e0 + LANES * j, LANES)] = b[j]
        at = pl.ds(e0, ec)
        p1 = dot(kbd, qs[:, at])
        p2 = dot(k2bd, ws[:, at])
        c = c_ref[:, at]
        beta = beta_ref[:, at]
        eps = beta / (1.0 + beta * ksum)
        dy = dy_ref[:, at]
        deps_ref[pl.ds(base, BT), at] = (c * jax.nn.sigmoid(c)) * p1 - p2
        dxc_ref[pl.ds(base, BT), at] = dy * skip_ref[:, at] + eps * p1
        r1 = r1 + dot_nt(us_ref[:, at].astype(BF), qs[:, at])
        r2 = r2 + dot_nt(eps.astype(BF), ws[:, at])
        r3 = r3 + dot_nt(dy.astype(BF), s_ref[:, at])
    same = iota((BT, BT * N), 0) == iota((BT, BT * N), 1) // N
    gather_k = (iota((BT * N, LANES), 1) == rank + iota((BT * N, LANES), 0) % N).astype(F32)
    gather_q = (iota((BT * N, LANES), 1) == rank + N + iota((BT * N, LANES), 0) % N).astype(F32)

    def pick(r, g):
        return jnp.dot(jnp.where(same, r, 0.0), g, precision=lax.Precision.HIGHEST, preferred_element_type=F32)

    dkq_ref[pl.ds(base, BT), :] = pick(r1, gather_k) - 2.0 * pf * pick(r2, gather_k) + pick(r3, gather_q)

    @pl.when(i == steps - 1)
    def _():
        projw = proj_ref[...]
        pw = projw.astype(F32)
        colw = iota((t_len, LANES), 1)
        isk = (colw >= rank) & (colw < rank + N)
        kall = jnp.where(isk, pw, 0.0)
        ks = jnp.sum(kall * kall, axis=-1, keepdims=True)
        tc = 256

        def first(k, carry):
            dkc, ddt = carry
            at = pl.ds(pl.multiple_of(k * tc, tc), tc)
            beta = beta_all[:, at]
            inv = 1.0 / (1.0 + beta * ks)
            dq = deps_ref[:, at] * (inv * inv)
            dkc = dkc + jnp.sum(dq * beta * beta, axis=-1, keepdims=True)
            dp = (dq * beta * (1.0 - beta)).astype(BF)
            gdtb_ref[:, at] = jnp.sum(dp.astype(F32), axis=0, keepdims=True)
            gdt_ref[:, at] = dot_tn(projw, dp)
            ddt = ddt + dot_nt(dp, dtp_ref[:, at])
            return dkc, ddt

        dkc, ddt = lax.fori_loop(
            0, inner // tc, first, (jnp.zeros((t_len, 1), F32), jnp.zeros((t_len, LANES), F32)))
        dproj = (jnp.where(colw < rank, ddt, dkq_ref[...]) - 2.0 * kall * dkc).astype(BF)
        mask = mask_ref[...]
        lead = xi_ref.shape[0] - t_len

        def second(k, carry):
            at = pl.ds(pl.multiple_of(k * tc, tc), tc)
            c = c_all[:, at]
            act, der = silu_parts(c)
            gxp_ref[at, :] = dot_tn(act.astype(BF), dproj)
            dc = (dxc_ref[:, at] + dot_nt(dproj, xp_ref[at, :])) * der
            gcb_ref[:, at] = jnp.sum(dc, axis=0, keepdims=True)
            xi = xi_ref[:, at]
            pad = jnp.zeros((8, tc), F32)
            dxi = ck_ref[3:4, at] * dc
            rim = jnp.zeros((8, tc), F32)
            gck_ref[3:4, at] = jnp.sum(dc * xi[lead:], axis=0, keepdims=True)
            for j in range(3):
                m = dc * mask[:, j : j + 1]
                gck_ref[j : j + 1, at] = jnp.sum(m * xi[lead - 3 + j : lead - 3 + j + t_len], axis=0, keepdims=True)
                m = m * ck_ref[j : j + 1, at]
                ext = jnp.concatenate([pad, m, pad], axis=0)
                dxi = dxi + ext[8 + 3 - j : 8 + 3 - j + t_len]
                rim = rim + ext[8 - j : 16 - j]
            dxi_ref[:, at] = dxi
            rim_ref[:, at] = jnp.where(iota((8, tc), 0) < 3, rim, 0.0)
            return carry

        lax.fori_loop(0, inner // tc, second, 0)


def bwd_b(rank, fa, fb, dy, bin_, w, mask):
    t_len = dy.shape[0]
    inner = w["cb"].shape[1]
    steps = t_len // BT

    def blk(r, c):
        return pl.BlockSpec((r, c), lambda i: (steps - 1 - i, 0))

    def whole(r, c):
        return pl.BlockSpec((r, c), lambda i: (0, 0))

    def sd(*s):
        return jax.ShapeDtypeStruct(s, F32)

    ext = fa["xi"].shape[0]
    return pl.pallas_call(
        functools.partial(bwd_b_kernel, rank),
        grid=(steps,),
        in_specs=[
            blk(BT * N, LANES), blk(BT * N, LANES), blk(BT, LANES), blk(BT, inner), blk(BT, inner), blk(BT, inner),
            blk(BT, inner), blk(BT, inner), blk(BT * N, inner), blk(BT, inner),
            whole(N, inner), whole(t_len, LANES), whole(1, inner), whole(t_len, inner), whole(t_len, inner),
            whole(ext, inner), whole(8, inner), whole(inner, LANES), whole(LANES, inner), whole(t_len, LANES),
        ],
        out_specs=[
            whole(t_len, inner), whole(8, inner), whole(LANES, inner), whole(1, inner), whole(inner, LANES),
            whole(1, inner), whole(8, inner),
        ],
        out_shape=[
            sd(t_len, inner), sd(8, inner), sd(LANES, inner), sd(1, inner), sd(inner, LANES), sd(1, inner), sd(8, inner),
        ],
        scratch_shapes=[
            pltpu.VMEM((N, inner), F32), pltpu.VMEM((BT * N, inner), BF), pltpu.VMEM((BT * N, inner), BF),
            pltpu.VMEM((t_len, inner), F32), pltpu.VMEM((t_len, inner), F32), pltpu.VMEM((t_len, LANES), F32),
            pltpu.VMEM((8, LANES), BF),
        ],
        compiler_params=params(),
        name="back_scan",
    )(
        fa["k2"], fa["qb"], fa["proj"], fa["ex"], fa["us"], dy, fa["beta"], fa["c"], fb["s"], fb["sb"],
        bin_, fa["proj"], w["skip"], fa["beta"], fa["c"], fa["xi"], w["ck"], w["xp"], w["dtp"], mask,
    )


def bwd_c_kernel(
    layer, dxi_ref, rim_ref, dz_ref, u_ref, h_ref, gout_ref, gain_ref, in_own, in_oth,
    gx_ref, dh_ref, ggain_ref,
    w_buf, sems,
):
    t_len, width = h_ref.shape
    inner = dz_ref.shape[1]
    cb = 512
    n_chunk = 2 * inner // cb
    for k in range(n_chunk):
        at = pl.ds(k * cb, cb)
        chosen_copy(layer, in_own.at[:, at], in_oth.at[:, at], w_buf.at[:, at], sems.at[k])
    u = u_ref[...]
    du = jnp.zeros((t_len, width), F32)
    for k in range(n_chunk):
        at = pl.ds(k * cb, cb)
        if k < inner // cb:
            dxi = dxi_ref[:, at]
            rim = jnp.concatenate([jnp.zeros((5, cb), F32), rim_ref[0:3, at]], axis=0)
            g = jnp.concatenate([dxi[: t_len - 8], dxi[t_len - 8 :] + rim], axis=0).astype(BF)
            gx_ref[:, at] = dot_tn(u, g).astype(BF)
        else:
            g = dz_ref[:, pl.ds(k * cb - inner, cb)]
        wait_copy(in_own.at[:, at], w_buf.at[:, at], sems.at[k])
        du = du + dot_nt(g, w_buf[:, at])
    hf = h_ref[...].astype(F32)
    inv = lax.rsqrt(jnp.mean(hf * hf, axis=-1, keepdims=True) + NORM_EPS)
    unit = hf * inv
    ggain_ref[...] = jnp.sum(du * unit, axis=0, keepdims=True)
    dn = du * gain_ref[...]
    dh = gout_ref[...].astype(F32) + inv * (dn - unit * jnp.mean(dn * unit, axis=-1, keepdims=True))
    dh_ref[...] = dh.astype(BF)


def bwd_c(layer, dxi, rim, dz, fa, h, gout, w, in_own, in_oth):
    t_len, width = h.shape
    inner = dz.shape[1]
    return pl.pallas_call(
        functools.partial(bwd_c_kernel, layer),
        out_shape=[
            jax.ShapeDtypeStruct((width, inner), BF), jax.ShapeDtypeStruct((t_len, width), BF),
            jax.ShapeDtypeStruct((1, width), F32),
        ],
        in_specs=[VSPEC] * 7 + [ANYSPEC] * 2,
        out_specs=[VSPEC] * 3,
        scratch_shapes=[pltpu.VMEM((width, 2 * inner), BF), pltpu.SemaphoreType.DMA((2 * inner // 512,))],
        compiler_params=params(),
        name=f"back_in_{layer}",
    )(dxi, rim, dz, fa["u"], h, gout, w["gain"], in_own, in_oth)


def bit_orders(bits):
    low = list(range(bits))
    return [low, [1, 0] + low[2:], [2, 0, 1] + low[3:], low]


def sum_kernel(layer, bits, orders, *refs):
    cnt = len(orders)
    srcs = refs[:cnt]
    outs = refs[cnt : 2 * cnt]
    accs = refs[2 * cnt : 3 * cnt]
    sib = refs[3 * cnt : 4 * cnt]
    rest = refs[4 * cnt :]
    recvs = [rest[p * bits : (p + 1) * bits] for p in range(cnt)]
    res = rest[cnt * bits : cnt * bits + cnt]
    load_sem, ssem, rsem, fsem, frsem = rest[cnt * bits + cnt :]
    sec = lax.axis_index("section")
    me = lax.axis_index("ctx")
    my_bit = [lax.rem(me // 2**b, 2) for b in range(bits)]
    barrier = pltpu.get_barrier_semaphore()
    pl.semaphore_signal(barrier, inc=1, device_id=(1 - sec, me), device_id_type=MESH)
    for b in range(bits):
        to = me + 2**b * (1 - 2 * my_bit[b])
        pl.semaphore_signal(barrier, inc=1, device_id=(sec, to), device_id_type=MESH)
    pl.semaphore_wait(barrier, bits + 1)

    def half(p, which):
        lanes = srcs[p].shape[-1] // 2
        return srcs[p].at[(slice(None),) * (bits + 1) + (pl.ds(pl.multiple_of(which * lanes, LANES), lanes),)]

    def across(p):
        return pltpu.make_async_remote_copy(
            src_ref=half(p, 1 - sec), dst_ref=sib[p], send_sem=ssem.at[p, 0], recv_sem=rsem.at[p, 0],
            device_id=(1 - sec, me), device_id_type=MESH)

    def load(p):
        return pltpu.make_async_copy(half(p, sec), accs[p], load_sem.at[p])

    def index(p, r, last):
        idx = [slice(None)] * bits
        for q in range(r):
            b = orders[p][q]
            idx[bits - 1 - b] = my_bit[b]
        b = orders[p][r]
        idx[bits - 1 - b] = last if last is not None else my_bit[b]
        return tuple(idx)

    def step(p, r):
        b = orders[p][r]
        to = me + 2**b * (1 - 2 * my_bit[b])
        return pltpu.make_async_remote_copy(
            src_ref=accs[p].at[index(p, r, 1 - my_bit[b])], dst_ref=recvs[p][r],
            send_sem=ssem.at[p, r + 1], recv_sem=rsem.at[p, r + 1],
            device_id=(sec, to), device_id_type=MESH)

    for p in range(cnt):
        across(p).start()
        load(p).start()

    def add(p, r):
        if r == 0:
            across(p).wait_recv()
            load(p).wait()
            rows = accs[p].shape[-2]
            lead = accs[p].shape[:bits]
            total = math.prod(lead)

            def body(k, carry):
                idx = tuple(lax.rem(k // 2 ** (bits - 1 - d), 2) for d in range(bits))
                accs[p][idx] = (accs[p][idx].astype(F32) + sib[p][idx].astype(F32)).astype(BF)
                return carry

            lax.fori_loop(0, total, body, 0)
            return
        step(p, r - 1).wait_recv()
        shape = recvs[p][r - 1].shape[:-2]
        total = math.prod(shape)
        fixed = index(p, r - 1, None)

        def body(k, carry):
            sub = []
            left = len(shape)
            for d in range(len(shape)):
                left -= 1
                sub.append(lax.rem(k // 2**left, 2))
            full, pos = [], 0
            for f in fixed:
                if isinstance(f, slice):
                    full.append(sub[pos])
                    pos += 1
                else:
                    full.append(f)
            val = accs[p][tuple(full)].astype(F32) + recvs[p][r - 1][tuple(sub)].astype(F32)
            if r == bits:
                res[p][...] = val
            else:
                accs[p][tuple(full)] = val.astype(BF)
            return carry

        lax.fori_loop(0, total, body, 0)

    for r in range(bits + 1):
        for p in range(cnt):
            add(p, r)
            if r < bits:
                step(p, r).start()

    def final(p):
        lanes = res[p].shape[-1]
        return pltpu.make_async_remote_copy(
            src_ref=res[p], dst_ref=outs[p].at[:, pl.ds(pl.multiple_of((1 - layer) * lanes, LANES), lanes)],
            send_sem=fsem.at[p], recv_sem=frsem.at[p], device_id=(1 - sec, me), device_id_type=MESH)

    @pl.when(sec != layer)
    def _():
        for p in range(cnt):
            final(p).start()
        for p in range(cnt):
            final(p).wait_send()

    @pl.when(sec == layer)
    def _():
        for p in range(cnt):
            lanes = res[p].shape[-1]
            outs[p][:, pl.ds(layer * lanes, lanes)] = res[p][...]
        for p in range(cnt):
            final(p).wait_recv()

    for p in range(cnt):
        across(p).wait_send()
        for r in range(bits):
            step(p, r).wait_send()


def summed(layer, n, cid, arrays):
    bits = n.bit_length() - 1
    orders = bit_orders(bits)[: len(arrays)]
    srcs, outs, accs, sibs, recvs, res = [], [], [], [], [], []
    for order, a in zip(orders, arrays):
        rows, lanes = a.shape[0] // n, a.shape[1]
        srcs.append(a.reshape((2,) * bits + (rows, lanes)))
        outs.append(jax.ShapeDtypeStruct((rows, lanes), F32))
        accs.append(pltpu.VMEM((2,) * bits + (rows, lanes // 2), BF))
        sibs.append(pltpu.VMEM((2,) * bits + (rows, lanes // 2), BF))
        for r in range(bits):
            recvs.append(pltpu.VMEM((2,) * (bits - 1 - r) + (rows, lanes // 2), BF))
        res.append(pltpu.VMEM((rows, lanes // 2), F32))
    cnt = len(arrays)
    return pl.pallas_call(
        functools.partial(sum_kernel, layer, bits, orders),
        out_shape=outs,
        in_specs=[ANYSPEC] * cnt,
        out_specs=[VSPEC] * cnt,
        scratch_shapes=accs + sibs + recvs + res + [
            pltpu.SemaphoreType.DMA((cnt,)), pltpu.SemaphoreType.DMA((cnt, bits + 1)),
            pltpu.SemaphoreType.DMA((cnt, bits + 1)), pltpu.SemaphoreType.DMA((cnt,)), pltpu.SemaphoreType.DMA((cnt,)),
        ],
        compiler_params=params(collective_id=cid, has_side_effects=True),
        name=f"sums_{layer}",
    )(*srcs)


def shift(value, axis, by):
    size = lax.axis_size(axis)
    return lax.ppermute(value, axis, [(i, i + by) for i in range(size) if 0 <= i + by < size])


def starts_of(position, bounds_row):
    start = jnp.zeros(position.shape, jnp.int32)
    for cut in range(1, 7):
        start = jnp.where(position >= bounds_row[cut], bounds_row[cut], start)
    return start


def pack_small(n, gain, ck, cb, xp, dt, dtb, skip):
    flat = [
        gain.reshape(n, -1),
        ck.reshape(ck.shape[0], n, -1).transpose(1, 0, 2).reshape(n, -1),
        cb.reshape(n, -1), dtb.reshape(n, -1), skip.reshape(n, -1),
        xp.reshape(n, -1), dt.reshape(n, -1),
    ]
    sizes = [f.shape[1] for f in flat]
    total = sum(sizes)
    unit = 16 * 2 * LANES
    padded = -(-total // unit) * unit
    flat.append(jnp.zeros((n, padded - total), F32))
    return jnp.concatenate(flat, axis=1).astype(BF).reshape(n * (padded // (2 * LANES)), 2 * LANES), sizes


def on_device(
    tokens, cotangent, bounds, norm_gain, in_proj, conv_kernel, conv_bias, x_proj, dt_proj, dt_bias, skip_gain, out_proj
):
    sec = lax.axis_index("section")
    n = lax.axis_size("ctx")
    me = lax.axis_index("ctx")
    t_len = tokens.shape[1]
    rank = dt_proj.shape[1]
    inner = in_proj.shape[2] // 2
    used = x_proj.shape[2]

    def swap(v):
        return lax.ppermute(v, "section", [(0, 1), (1, 0)])

    small = jnp.concatenate(
        [
            norm_gain[0].reshape(-1), conv_kernel[0].reshape(-1), conv_bias[0].reshape(-1), dt_bias[0].reshape(-1),
            skip_gain[0].reshape(-1), x_proj[0].reshape(-1), dt_proj[0].reshape(-1),
        ]
    )
    in_own, out_own = in_proj[0], out_proj[0]
    in_oth, small_oth, out_oth = swap(in_own), swap(small), swap(out_own)
    weights = []
    for layer in range(2):
        v = jnp.where(sec == layer, small, small_oth)
        at = 0

        def take(shape):
            nonlocal at
            size = math.prod(shape)
            piece = v[at : at + size].reshape(shape)
            at += size
            return piece

        w = {"gain": take((1, tokens.shape[2])).astype(F32)}
        w["ck"] = jnp.pad(take((4, inner)).astype(F32), ((0, 4), (0, 0)))
        w["cb"] = take((1, inner)).astype(F32)
        w["dtb"] = take((1, inner)).astype(F32)
        w["skip"] = take((1, inner)).astype(F32)
        w["xp"] = jnp.pad(take((inner, used)), ((0, 0), (0, LANES - used)))
        w["dtp"] = jnp.pad(take((rank, inner)), ((0, LANES - rank), (0, 0)))
        weights.append(w)
    tok = lax.dynamic_index_in_dim(tokens, sec, 0, keepdims=False)
    cot = lax.dynamic_index_in_dim(cotangent, sec, 0, keepdims=False)
    row = lax.dynamic_index_in_dim(bounds, sec, 0, keepdims=False)
    position = me * t_len + jnp.arange(t_len, dtype=jnp.int32)
    start = starts_of(position, row)
    marks = [(position - 3 + j >= start).astype(F32) for j in range(4)] + [(position != start).astype(F32)]
    mask = jnp.pad(jnp.stack(marks, axis=1), ((0, 0), (0, LANES - 5)))

    names_a = ("u", "xi", "z", "c", "proj", "beta", "ex", "us", "k2", "kb", "qb", "summ")
    names_b = ("s", "sb", "y", "o", "h")
    h = tok
    saved = []
    for layer in range(2):
        w = weights[layer]
        rim = shift(h[t_len - 16 :], "ctx", 1)
        fa = dict(zip(names_a, fwd_a(layer, rank, h, rim, w, mask, in_own, in_oth)))
        sin, dec = carry(n, False, 1 + layer, fa["summ"])
        fb = dict(zip(names_b, fwd_b(layer, rank, h, fa, sin, w, out_own, out_oth)))
        saved.append((h, fa, fb, dec))
        h = fb["h"]
    block_out = h
    gout = cot
    sums = [None, None]
    for layer in (1, 0):
        w = weights[layer]
        hin, fa, fb, dec = saved[layer]
        dy, dz, go, gz, gskip, frm = bwd_a(layer, gout, fa, fb, w, out_own, out_oth)
        (bin_,) = carry(n, True, 3 + layer, frm, dec)
        dxi, rim, gdt, gdtb, gxp, gcb, gck = bwd_b(rank, fa, fb, dy, bin_, w, mask)
        rim = shift(rim, "ctx", -1)
        gx, dh, ggain = bwd_c(layer, dxi, rim, dz, fa, hin, gout, w, in_own, in_oth)
        packed, sizes = pack_small(n, ggain, gck[:4], gcb, gxp, gdt[:rank], gdtb, gskip)
        sums[layer] = summed(layer, n, 5 + layer, (gx, gz, go, packed))
        gout = dh

    def mine(k):
        return jnp.where(sec == 0, sums[0][k], sums[1][k])

    s_small = mine(3).reshape(-1)
    parts, at = [], 0
    for size in sizes:
        parts.append(s_small[at : at + size])
        at += size
    g_gain, g_ck, g_cb, g_dtb, g_skip, g_xp, g_dt = parts
    return (
        block_out[None],
        gout[None],
        g_gain[None],
        jnp.concatenate([mine(0), mine(1)], axis=1)[None],
        g_ck.reshape(1, 4, -1),
        g_cb[None],
        g_xp.reshape(1, -1, LANES)[:, :, :used],
        g_dt.reshape(1, -1, inner),
        g_dtb[None],
        g_skip[None],
        mine(2)[None],
    )


def solution(mesh):
    placed = (
        P(None, "ctx", None), P(None, "ctx", None), P(), P("section", None), P("section", None, None),
        P("section", None, None), P("section", None), P("section", None, None), P("section", None, None),
        P("section", None), P("section", None), P("section", None, None),
    )
    return jax.shard_map(
        on_device,
        mesh=mesh,
        in_specs=placed,
        out_specs=(
            P("section", "ctx", None), P("section", "ctx", None), P("section", "ctx"), P("section", "ctx", None),
            P("section", None, "ctx"), P("section", "ctx"), P("section", "ctx", None), P("section", "ctx", None),
            P("section", "ctx"), P("section", "ctx"), P("section", "ctx", None),
        ),
        check_vma=False,
    )
```

time: 3170 us -> 457 us (0.14)
  waiting for transfers between devices: 1260 us -> 0.89 us
  matrix products: 744 us -> 0 us
  other arithmetic: 616 us -> 21.7 us
  Pallas kernels: 0 us -> 386 us
  local copies, waits for them, and re-layouts: 270 us -> 27 us
  loops' own time: 90.9 us -> 0 us
  blocking collectives: 74.1 us -> 0 us
  between operations: 46.6 us -> 1.65 us
    dot_general x129 -> x0, matrix products: 744 us -> none  [the longest x48 398 us: block_states(): jnp.dot(within_blk, (jnp.exp(-cumulative) * source).reshape(length, -1),...]
    all_gather x15 -> x0, waiting for transfers between devices: 684 us -> none  [carried_in(): lax.all_gather(part.astype(kind), axis)]
    reduce_scatter x3 -> x0, waiting for transfers between devices: 564 us -> none  [the longest x1 352 us: on_device(): lax.psum_scatter(grad_in, 'ctx', scatter_dimension=0, tiled=True)]
    pallas_call x0 -> x16, Pallas kernels: none -> 386 us  [the longest x2 166 us: summed(): pl.pallas_call(functools.partial(sum_kernel, layer, bits, orders), out_sh...]
    another operation x90 -> x10, other arithmetic: 223 us -> 6.25 us  [the longest x48 188 us: block_states(): cumulative = jnp.cumsum(log_decay(step_blk, key_blk), axis=0)]
    select_n x147 -> x2, other arithmetic: 140 us -> 1.41 us  [the longest x1 1.31 us: mine(): return jnp.where(sec == 0, sums[0][k], sums[1][k])]
    another operation x27 -> x0, loops' own time: 90.9 us -> none  [the longest x9 85.5 us: run_states(): lax.scan(jax.checkpoint(block_states), start_state, pieces)]
    unnamed x1 -> x0, blocking collectives: 74.1 us -> none
  transfers between devices with their start and end apart: 34 -> 7, of which waited for: 23 -> 1; matrix products, arithmetic and copies ran while one was open for 23% -> 8% of each run, Pallas kernels for 0% -> 25%
where the time goes in v1:
time: 457 us; the launch traced here: 449 us
  Pallas kernels  386 us (84%)
  local copies, waits for them, and re-layouts  27 us (6%)
  other arithmetic  21.7 us (5%)
  starting transfers between devices  12 us (3%)
    pallas_call x2, Pallas kernels, summed(): pl.pallas_call(functools.partial(sum_kernel, layer, bits, orders), out_sh...  166 us
    pallas_call x4, Pallas kernels, carry(): pl.pallas_call(functools.partial(carry_kernel, n, reverse), out_shape=[go...  62 us
    pallas_call x2, Pallas kernels, bwd_b(): pl.pallas_call(functools.partial(bwd_b_kernel, rank), grid=(steps,), in_s...  52.5 us
    pallas_call x2, Pallas kernels, bwd_a(): pl.pallas_call(functools.partial(bwd_a_kernel, layer), out_shape=[sd(F32,...  31.5 us
    pallas_call x2, Pallas kernels, fwd_a(): pl.pallas_call(functools.partial(fwd_a_kernel, layer, rank), out_shape=[b...  29.9 us
    pallas_call x2, Pallas kernels, fwd_b(): pl.pallas_call(functools.partial(fwd_b_kernel, layer, rank), grid=(t_len...  26.5 us
    pallas_call x2, Pallas kernels, bwd_c(): pl.pallas_call(functools.partial(bwd_c_kernel, layer), out_shape=[jax.Sha...  17.7 us
    ppermute x4, starting transfers between devices, shift(): lax.ppermute(value, axis, [(i, i + by) for i in range(size) if 0 <= i + b...  11.3 us
  transfers between devices with their start and end apart: 7, of which 1 were waited for; matrix products, arithmetic and copies ran while one was open for 8% of the time, Pallas kernels for 25%

profile of v1, /device:TPU:0, one launch (start us, length us, event | category | flops | bytes accessed | tf_op | source)
XLA Modules:
  0.0 449.0 jit_solution(7808548620594562552)
XLA Ops:
  1.7 4.8 %collective-permute-start = (bf16[16,1024]{1,0:T(8,128)(2,1)S(1)}, bf16[16,1024]{1,0:T(8,128)(2,1)S(1)}, u32[]{:S(2)}, u32[]{:S(2)}) collective-permute-start(bf16[16,1024]{1,0:T(8,128)(2,1)S(1)} %dynamic-slice_bitcast_fusion.2), channel_id=1, source_target_pairs={{0,1},{1,2},{2,3},{3,4},{4,5},{5,6},{6,7},{7,8},{8,9},{9,10},{10,1... | collective-permute-start | bytes 98312 | tf_op jit(solution)/shard_map/ppermute | solution.py:837
  15.2 3.9 fusion.3
  27.8 14.9 %fwd_in_0.1 = (bf16[128,1024]{1,0:T(8,128)(2,1)}, f32[144,2048]{1,0:T(8,128)}, f32[128,2048]{1,0:T(8,128)}, f32[128,2048]{1,0:T(8,128)}, bf16[128,128]{1,0:T(8,1...) custom-call(bf16[128,1024]{1,0:T(8,128)(2,1)} %dynamic-slice_bitcast, ...), custom_call_target="tpu_custom_call" | custom-call | tf_op jit(solution)/shard_map/fwd_in_0/pallas_call | solution.py:171
  42.8 17.0 %carry_1.1 = (bf16[16,2048]{1,0:T(8,128)(2,1)}, bf16[16,16,128]{2,1,0:T(8,128)(2,1)}) custom-call(bf16[32,2048]{1,0:T(8,128)(2,1)} %get-tuple-element.96.refs_0_), custom_call_target="tpu_custom_call" | custom-call | tf_op jit(solution)/shard_map/carry_1/pallas_call | solution.py:286
  59.7 13.3 %fwd_out_0.1 = (bf16[2048,2048]{1,0:T(8,128)(2,1)}, bf16[128,2048]{1,0:T(8,128)(2,1)}, f32[128,2048]{1,0:T(8,128)}, bf16[128,2048]{1,0:T(8,128)(2,1)}, bf16[128,1024]{1,0:T(8,128)(2,1)}) custom-call(f32[2048,128]{1,0:T(8,128)} %get-tuple-element.89.k2_ref, f32[2048,128]{1,0:T(8,128)} %get-tuple-element.90.kb_ref, ...), custom_call_target="tpu_custom_call" | custom-call | tf_op jit(solution)/shard_map/fwd_out_0/pallas_call | solution.py:359
  73.8 3.4 collective-permute-start.4
  80.7 15.0 %fwd_in_1.1 = (bf16[128,1024]{1,0:T(8,128)(2,1)}, f32[144,2048]{1,0:T(8,128)}, f32[128,2048]{1,0:T(8,128)}, f32[128,2048]{1,0:T(8,128)}, bf16[128,128]{1,0:T(8,1...) custom-call(bf16[128,1024]{1,0:T(8,128)(2,1)} %get-tuple-element.98., ...), custom_call_target="tpu_custom_call" | custom-call | tf_op jit(solution)/shard_map/fwd_in_1/pallas_call | solution.py:171
  95.7 14.5 %carry_2.1 = (bf16[16,2048]{1,0:T(8,128)(2,1)}, bf16[16,16,128]{2,1,0:T(8,128)(2,1)}) custom-call(bf16[32,2048]{1,0:T(8,128)(2,1)} %get-tuple-element.106.refs_0_), custom_call_target="tpu_custom_call" | custom-call | tf_op jit(solution)/shard_map/carry_2/pallas_call | solution.py:286
  110.2 13.2 %fwd_out_1.1 = (bf16[2048,2048]{1,0:T(8,128)(2,1)}, bf16[128,2048]{1,0:T(8,128)(2,1)}, f32[128,2048]{1,0:T(8,128)}, bf16[128,2048]{1,0:T(8,128)(2,1)}, bf16[128,1024]{1,0:T(8,128)(2,1)}) custom-call(f32[2048,128]{1,0:T(8,128)} %get-tuple-element.99.k2_ref, f32[2048,128]{1,0:T(8,128)} %get-tuple-element.100.kb_ref, ...), custom_call_target="tpu_custom_call" | custom-call | tf_op jit(solution)/shard_map/fwd_out_1/pallas_call | solution.py:359
  123.4 15.8 %back_out_1.1 = (f32[128,2048]{1,0:T(8,128)}, bf16[128,2048]{1,0:T(8,128)(2,1)}, bf16[2048,1024]{1,0:T(8,128)(2,1)}, bf16[1024,2048]{1,0:T(8,128)(2,1)}, f32[1,2048]{1,0:T(1,128)}, /*index=5*/bf16[16,2048]{1,0:T(8,128)(2,1)}) custom-call(bf16[128,1024]{1,0:T(8,128)(2,1)} %dynamic-slice_bitcast_fusion.gout_ref, f32[128,2048]{1,0:T(8,128)} %get-tuple-element.105.z_ref, ...), custom_call_target="tpu_custom_call" | custom-call | tf_op jit(solution)/shard_map/back_out_1/pallas_call | solution.py:442
  139.2 14.7 %carry_4.1.bin_ref = bf16[16,2048]{1,0:T(8,128)(2,1)} custom-call(bf16[16,2048]{1,0:T(8,128)(2,1)} %get-tuple-element.118.refs_0_, bf16[16,16,128]{2,1,0:T(8,128)(2,1)} %get-tuple-element.119.refs_1_), custom_call_target="tpu_custom_call" | custom-call | tf_op jit(solution)/shard_map/carry_4/pallas_call | solution.py:286
  153.9 26.2 %back_scan.2 = (f32[128,2048]{1,0:T(8,128)}, f32[8,2048]{1,0:T(8,128)}, f32[128,2048]{1,0:T(8,128)}, f32[1,2048]{1,0:T(1,128)}, f32[2048,128]{1,0:T(8,128)}, /*index=5*/f32[1,2048]{1,0:T(1,128)}, f32[8,2048]{1,0:T(8,128)}) custom-call(f32[2048,128]{1,0:T(8,128)} %get-tuple-element.99.k2_ref, f32[2048,128]{1,0:T(8,128)} %get-tuple-element.110.qb_ref, ...), custom_call_target="tpu_custom_call" | custom-call | tf_op jit(solution)/shard_map/back_scan/pallas_call | solution.py:594
  180.1 1.5 collective-permute-start.5
  184.0 1.3 convert.97
  187.4 8.8 %back_in_1.1 = (bf16[1024,2048]{1,0:T(8,128)(2,1)}, bf16[128,1024]{1,0:T(8,128)(2,1)}, f32[1,1024]{1,0:T(1,128)}) custom-call(f32[128,2048]{1,0:T(8,128)} %get-tuple-element.121.dxi_ref, f32[8,2048]{1,0:T(8,128)} %copy-done.9, bf16[128,2048]{1,0:T(8,128)(2,1)} %get-tuple-element.123.dz_ref, bf16[128,1024]{1,0:T(8,128)(2,1)} %get-tuple-element.113.u_ref, ...), custom_call_target="tpu_custom_call" | custom-call | tf_op jit(solution)/shard_map/back_in_1/pallas_call | solution.py:660
  196.2 15.8 %back_out_0.1 = (f32[128,2048]{1,0:T(8,128)}, bf16[128,2048]{1,0:T(8,128)(2,1)}, bf16[2048,1024]{1,0:T(8,128)(2,1)}, bf16[1024,2048]{1,0:T(8,128)(2,1)}, f32[1,2048]{1,0:T(1,128)}, /*index=5*/bf16[16,2048]{1,0:T(8,128)(2,1)}) custom-call(bf16[128,1024]{1,0:T(8,128)(2,1)} %get-tuple-element.124.gout_ref, f32[128,2048]{1,0:T(8,128)} %get-tuple-element.95.z_ref, ...), custom_call_target="tpu_custom_call" | custom-call | tf_op jit(solution)/shard_map/back_out_0/pallas_call | solution.py:442
  212.0 15.9 %carry_3.1.bin_ref = bf16[16,2048]{1,0:T(8,128)(2,1)} custom-call(bf16[16,2048]{1,0:T(8,128)(2,1)} %get-tuple-element.132.refs_0_, bf16[16,16,128]{2,1,0:T(8,128)(2,1)} %get-tuple-element.133.refs_1_), custom_call_target="tpu_custom_call" | custom-call | tf_op jit(solution)/shard_map/carry_3/pallas_call | solution.py:286
  227.9 26.3 %back_scan.3 = (f32[128,2048]{1,0:T(8,128)}, f32[8,2048]{1,0:T(8,128)}, f32[128,2048]{1,0:T(8,128)}, f32[1,2048]{1,0:T(1,128)}, f32[2048,128]{1,0:T(8,128)}, /*index=5*/f32[1,2048]{1,0:T(1,128)}, f32[8,2048]{1,0:T(8,128)}) custom-call(f32[2048,128]{1,0:T(8,128)} %get-tuple-element.89.k2_ref, f32[2048,128]{1,0:T(8,128)} %get-tuple-element.109.qb_ref, ...), custom_call_target="tpu_custom_call" | custom-call | tf_op jit(solution)/shard_map/back_scan/pallas_call | solution.py:594
  254.2 1.5 collective-permute-start.6
  258.0 1.3 convert.90
  262.9 82.2 %sums_1.1 = (f32[64,2048]{1,0:T(8,128)}, f32[64,2048]{1,0:T(8,128)}, f32[128,1024]{1,0:T(8,128)}, f32[112,256]{1,0:T(8,128)}) custom-call(bf16[2,2,2,2,64,2048]{5,4,3,2,1,0:T(8,128)(2,1)} %bitcast.102, bf16[2,2,2,2,64,2048]{5,4,3,2,1,0:T(8,128)(2,1)} %bitcast.99, bf16[2,2,2,2,128,1024]{5,4,3,2,1,0:T(8,128)(2,1)} %bitcast.98, ...), custom_call_target="tpu_custom_call" | custom-call | tf_op jit(solution)/shard_map/sums_1/pallas_call | solution.py:821
  345.8 8.9 %back_in_0.1 = (bf16[1024,2048]{1,0:T(8,128)(2,1)}, bf16[128,1024]{1,0:T(8,128)(2,1)}, f32[1,1024]{1,0:T(1,128)}) custom-call(f32[128,2048]{1,0:T(8,128)} %get-tuple-element.135.dxi_ref, f32[8,2048]{1,0:T(8,128)} %copy-done.8, bf16[128,2048]{1,0:T(8,128)(2,1)} %get-tuple-element.137.dz_ref, bf16[128,1024]{1,0:T(8,128)(2,1)} %get-tuple-element.127.u_ref, ...), custom_call_target="tpu_custom_call" | custom-call | tf_op jit(solution)/shard_map/back_in_0/pallas_call | solution.py:660
  357.4 83.5 %sums_0.1 = (f32[64,2048]{1,0:T(8,128)}, f32[64,2048]{1,0:T(8,128)}, f32[128,1024]{1,0:T(8,128)}, f32[112,256]{1,0:T(8,128)}) custom-call(bf16[2,2,2,2,64,2048]{5,4,3,2,1,0:T(8,128)(2,1)} %bitcast.103, bf16[2,2,2,2,64,2048]{5,4,3,2,1,0:T(8,128)(2,1)} %bitcast.101, bf16[2,2,2,2,128,1024]{5,4,3,2,1,0:T(8,128)(2,1)} %bitcast.100, ...), custom_call_target="tpu_custom_call" | custom-call | tf_op jit(solution)/shard_map/sums_0/pallas_call | solution.py:821
  445.3 1.3 broadcast_select_fusion.2
  (124 shorter events, 42.4 us)
Async XLA Ops:
  0.6 1.1 copy-start
  0.7 20.0 %copy-start.6 = (bf16[2,128,1024]{2,1,0:T(8,128)(2,1)S(1)}, bf16[2,128,1024]{2,1,0:T(8,128)(2,1)}, u32[]{:S(2)}) copy-start(bf16[2,128,1024]{2,1,0:T(8,128)(2,1)} %param.13) | copy-start | bytes 1572868
  1.7 25.2 %collective-permute-start = (bf16[16,1024]{1,0:T(8,128)(2,1)S(1)}, bf16[16,1024]{1,0:T(8,128)(2,1)S(1)}, u32[]{:S(2)}, u32[]{:S(2)}) collective-permute-start(bf16[16,1024]{1,0:T(8,128)(2,1)S(1)} %dynamic-slice_bitcast_fusion.2), channel_id=1, source_target_pairs={{0,1},{1,2},{2,3},{3,4},{4,5},{5,6},{6,7},{7,8},{8,9},{9,10},{10,1... | collective-permute-start | bytes 98312 | tf_op jit(solution)/shard_map/ppermute | solution.py:837
  13.3 8.1 %collective-permute-start.1 = (bf16[343040]{0:T(1024)(128)(2,1)S(1)}, bf16[343040]{0:T(1024)(128)(2,1)S(1)}, u32[]{:S(2)}, u32[]{:S(2)}) collective-permute-start(bf16[343040]{0:T(1024)(128)(2,1)S(1)} %constant_dynamic-update-slice_fusion), channel_id=1, source_target_pairs={{0,16},{16,0},{1,17},{17,1},{2,18},{18,2},{3,19},{19,3},{4,20},{20... | collective-permute-start | bytes 2058248 | tf_op jit(solution)/shard_map/ppermute | solution.py:874
  13.3 14.5 %collective-permute-start.2 = (bf16[1024,4096]{1,0:T(8,128)(2,1)}, bf16[1024,4096]{1,0:T(8,128)(2,1)}, u32[]{:S(2)}, u32[]{:S(2)}) collective-permute-start(bf16[1024,4096]{1,0:T(8,128)(2,1)} %bitcast.88), channel_id=1, source_target_pairs={{0,16},{16,0},{1,17},{17,1},{2,18},{18,2},{3,19},{19,3},{4,20},{20... | collective-permute-start | bytes 25165832 | tf_op jit(solution)/shard_map/ppermute | solution.py:874
  13.8 45.9 %collective-permute-start.3 = (bf16[2048,1024]{1,0:T(8,128)(2,1)}, bf16[2048,1024]{1,0:T(8,128)(2,1)}, u32[]{:S(2)}, u32[]{:S(2)}) collective-permute-start(bf16[2048,1024]{1,0:T(8,128)(2,1)} %bitcast.93), channel_id=1, source_target_pairs={{0,16},{16,0},{1,17},{17,1},{2,18},{18,2},{3,19},{19,3},{4,20},{20... | collective-permute-start | bytes 12582920 | tf_op jit(solution)/shard_map/ppermute | solution.py:874
  26.9 0.9 copy-start.10
  73.8 6.3 %collective-permute-start.4 = (bf16[16,1024]{1,0:T(8,128)(2,1)S(1)}, bf16[16,1024]{1,0:T(8,128)(2,1)S(1)}, u32[]{:S(2)}, u32[]{:S(2)}) collective-permute-start(bf16[16,1024]{1,0:T(8,128)(2,1)S(1)} %slice.136), channel_id=1, source_target_pairs={{0,1},{1,2},{2,3},{3,4},{4,5},{5,6},{6,7},{7,8},{8,9},{9,10},{10,1... | collective-permute-start | bytes 98312 | tf_op jit(solution)/shard_map/ppermute | solution.py:837
  80.1 0.6 copy-start.11
  153.9 32.9 %copy-start.13 = (f32[1,2048]{1,0:T(1,128)S(1)}, f32[1,2048]{1,0:T(1,128)}, u32[]{:S(2)}) copy-start(f32[1,2048]{1,0:T(1,128)} %get-tuple-element.157) | copy-start | bytes 24580
  180.1 6.7 %collective-permute-start.5 = (f32[8,2048]{1,0:T(8,128)}, f32[8,2048]{1,0:T(8,128)S(1)}, u32[]{:S(2)}, u32[]{:S(2)}) collective-permute-start(f32[8,2048]{1,0:T(8,128)} %get-tuple-element.122), channel_id=1, source_target_pairs={{1,0},{2,1},{3,2},{4,3},{5,4},{6,5},{7,6},{8,7},{9,8},{10,9},{11,1... | collective-permute-start | bytes 196616 | tf_op jit(solution)/shard_map/ppermute | solution.py:837
  186.8 0.6 copy-start.9
  227.9 32.9 %copy-start.14 = (f32[1,1024]{1,0:T(1,128)S(1)}, f32[1,1024]{1,0:T(1,128)}, u32[]{:S(2)}) copy-start(f32[1,1024]{1,0:T(1,128)} %get-tuple-element.153) | copy-start | bytes 12292
  254.2 91.0 %collective-permute-start.6 = (f32[8,2048]{1,0:T(8,128)}, f32[8,2048]{1,0:T(8,128)S(1)}, u32[]{:S(2)}, u32[]{:S(2)}) collective-permute-start(f32[8,2048]{1,0:T(8,128)} %get-tuple-element.136), channel_id=1, source_target_pairs={{1,0},{2,1},{3,2},{4,3},{5,4},{6,5},{7,6},{8,7},{9,8},{10,9},{11,1... | collective-permute-start | bytes 196616 | tf_op jit(solution)/shard_map/ppermute | solution.py:837
  262.9 82.2 %copy-start.12 = (f32[1,2048]{1,0:T(1,128)S(1)}, f32[1,2048]{1,0:T(1,128)}, u32[]{:S(2)}) copy-start(f32[1,2048]{1,0:T(1,128)} %get-tuple-element.146) | copy-start | bytes 24580
  345.2 0.6 copy-start.8
  357.4 83.6 %copy-start.7 = (f32[112,256]{1,0:T(8,128)S(1)}, f32[112,256]{1,0:T(8,128)}, u32[]{:S(2)}) copy-start(f32[112,256]{1,0:T(8,128)} %get-tuple-element.160) | copy-start | bytes 344068
  357.4 87.9 %copy-start.4 = (f32[64,2048]{1,0:T(8,128)S(1)}, f32[64,2048]{1,0:T(8,128)}, u32[]{:S(2)}) copy-start(f32[64,2048]{1,0:T(8,128)} %get-tuple-element.162) | copy-start | bytes 1572868
  357.4 87.9 %copy-start.5 = (f32[64,2048]{1,0:T(8,128)S(1)}, f32[64,2048]{1,0:T(8,128)}, u32[]{:S(2)}) copy-start(f32[64,2048]{1,0:T(8,128)} %get-tuple-element.164) | copy-start | bytes 1572868
  357.4 91.1 %copy-start.1 = (bf16[2,128,1024]{2,1,0:T(8,128)(2,1)S(1)}, bf16[2,128,1024]{2,1,0:T(8,128)(2,1)}, u32[]{:S(2)}) copy-start(bf16[2,128,1024]{2,1,0:T(8,128)(2,1)} %param.12) | copy-start | bytes 1572868
  440.9 6.7 %copy-start.2 = (f32[128,1024]{1,0:T(8,128)S(1)}, f32[128,1024]{1,0:T(8,128)}, u32[]{:S(2)}) copy-start(f32[128,1024]{1,0:T(8,128)} %get-tuple-element.166) | copy-start | bytes 1572868
  440.9 6.7 %copy-start.3 = (f32[128,1024]{1,0:T(8,128)S(1)}, f32[128,1024]{1,0:T(8,128)}, u32[]{:S(2)}) copy-start(f32[128,1024]{1,0:T(8,128)} %get-tuple-element.165) | copy-start | bytes 1572868
